TPU v7x, 128 devices: a whole 4x4x4 slice. The times are simulated.
128 devices in a mesh: bulk: 8 (over x, core), group: 16 (over z, y).
Axes of the slice: x: 4, y: 4, z: 4, core: 2. Of those that a mesh axis runs over, the one named last changes fastest.
Arguments:
- points: float32 [8, 786432], P(None, ('bulk', 'group')), may hold values from -6 to 6
- weights: float32 [64, 786432], P(None, ('bulk', 'group')), may hold values from -0.75 to 0.75
- leaf_order: int32 [786432], P(('bulk', 'group')), may hold values from 0 to 786431, as said below
- basis: float32 [3072, 256, 128], P(('bulk', 'group')), may hold values from -0.375 to 0.375
- transfer: float32 [3072, 128, 128], P(('bulk', 'group')), may hold values from -0.1875 to 0.1875
- skel_leaf: bfloat16 [3072, 8, 128], P(('bulk', 'group')), may hold values from -6 to 6
- skel_upper: bfloat16 [384, 8, 128], P(('bulk', 'group')), may hold values from -6 to 6
- near_list: int32 [3072, 12], P(('bulk', 'group')), may hold values from 0 to 3071, as said below
- leaf_interaction_list: int32 [3072, 32], P(('bulk', 'group')), may hold values from 0 to 3071, as said below
- far_upper: int32 [384, 32], P(('bulk', 'group')), may hold values from 0 to 383
Outputs:
- potential: float32 [64, 786432], P(None, ('bulk', 'group'))
Inputs may be any that keep to these rules, and one draw needn't show every extreme that they name: `leaf_order`: A permutation of the point indices. The 6144 positions of each device take exactly 384 points from the input shard of every device of the same group. `near_list`: entry 0 of each row is the leaf itself; every entry is within 24 leaves of the row's leaf. `leaf_interaction_list`: every entry lies in the same aligned block of 384 leaves as the row's leaf.
All inputs are finite; a program needn't handle non-finite values.
Results may differ from a plain program's by a relative error of at most 0.0041.
Values may be sent and summed in bfloat16 or wider, within the bound.
No kernel may reach another device: no remote copies, remote signals or barrier semaphores. Data moves between devices by JAX's collectives and lax.ppermute only.
A program may use at most 128 MiB of HBM per device.

v0:
```python
import functools
import math

import jax
import jax.numpy as jnp
from jax import lax
from jax.experimental import pallas as pl
from jax.experimental.pallas import tpu as pltpu
from jax.sharding import PartitionSpec as P

KIDS = 8

POINT_SCALE = math.sqrt(5.0) / 2.0 / math.log(2.0)
POLY_A = 3.0 / math.log(2.0)
POLY_B = 3.0 / math.log(2.0) ** 2
POLY_LOG = math.log2(math.log(2.0) ** 2 / 3.0)
AUG = 48
MIB = 1024 * 1024

f32 = jnp.float32
bf16 = jnp.bfloat16
TICK = jax.ShapeDtypeStruct((8, 128), f32)
NN = (((1,), (0,)), ((), ()))
NT = (((1,), (1,)), ((), ()))


def mm(a, b, dims=NN):
    return lax.dot_general(a, b, dims, preferred_element_type=f32)


def halves(x):
    high = x.astype(bf16)
    return high, (x - high.astype(f32)).astype(bf16)


def mm3(a, b):
    a_high, a_low = halves(a)
    b_high, b_low = halves(b)
    return mm(a_high, b_high) + (mm(a_high, b_low) + mm(a_low, b_high))


def squares(high, low):
    x = high + low
    norm = jnp.sum(x * x, axis=0, keepdims=True)
    first = norm.astype(bf16).astype(f32)
    second = (norm - first).astype(bf16).astype(f32)
    third = norm - first - second
    row = lax.broadcasted_iota(jnp.int32, high.shape, 0)
    parts = jnp.where(row % 3 == 0, first, jnp.where(row % 3 == 1, second, third))
    return row, parts


def source_rows(high, low):
    row, parts = squares(high, low)
    last = jnp.where(row < 3, 1.0, jnp.where(row < 6, parts, 0.0))
    high, low = -2.0 * high, -2.0 * low
    return jnp.concatenate([high, low, high, low, last, jnp.zeros_like(last)], axis=0).astype(bf16)


def target_rows(high, low):
    row, parts = squares(high, low)
    last = jnp.where(row < 3, parts, jnp.where(row < 6, 1.0, 0.0))
    rows = jnp.concatenate([high, high, low, low, last, jnp.zeros_like(last)], axis=0)
    return jnp.transpose(rows).astype(bf16)


def f32_halves(points):
    high, low = halves(points)
    return high.astype(f32), low.astype(f32)


def scaled_halves(points):
    return f32_halves(points.astype(f32) * POINT_SCALE)


def matern(square):
    square = jnp.maximum(square, 1e-30)
    t = square * lax.rsqrt(square)
    return (((t + POLY_A) * t + POLY_B) * jnp.exp2(POLY_LOG - t)).astype(bf16)


def index_body(order_ref, want_ref, src_ref, rank_ref, tick_ref):
    tick_ref[...] = jnp.zeros_like(tick_ref)
    group_count, _, pair = want_ref.shape
    lines = order_ref.shape[0]
    row_count = group_count * pair
    order = order_ref[...]
    owner = ((order.astype(f32) + 0.5) * (1.0 / row_count)).astype(jnp.int32)
    src = owner % group_count
    row = order - owner * row_count
    before = (
        lax.broadcasted_iota(jnp.int32, (128, 128), 0)
        < lax.broadcasted_iota(jnp.int32, (128, 128), 1)
    ).astype(f32).astype(bf16)
    above = (
        lax.broadcasted_iota(jnp.int32, (lines, lines), 1)
        < lax.broadcasted_iota(jnp.int32, (lines, lines), 0)
    ).astype(f32).astype(bf16)
    all_ones = jnp.ones((128, 128), bf16)
    rank = jnp.zeros(src.shape, f32)
    for g in range(group_count):
        here = src == g
        mask = here.astype(f32).astype(bf16)
        total = mm(mask, all_ones).astype(bf16)
        rank = jnp.where(here, mm(mask, before) + mm(above, total), rank)
    rank = rank.astype(jnp.int32)
    for i in range(lines // 2):
        for ref, x in ((src_ref, src), (rank_ref, rank)):
            ref[i] = jnp.concatenate([x[2 * i : 2 * i + 1], x[2 * i + 1 : 2 * i + 2]], axis=1)
    place = lax.broadcasted_iota(jnp.int32, (pair, 256), 0)
    owner = lax.broadcasted_iota(jnp.int32, (group_count, 256), 0)
    total = jnp.zeros((2 * group_count, pair), f32)
    for k in range(0, lines, 2):
        line = lambda x: jnp.concatenate([x[k : k + 1], x[k + 1 : k + 2]], axis=1)
        rank_line, src_line, row_line = line(rank), line(src), line(row)
        spots = (place == rank_line).astype(f32).astype(bf16)
        mine = owner == src_line
        high = jnp.where(mine, (row_line >> 7).astype(f32), 0.0)
        low = jnp.where(mine, (row_line & 127).astype(f32), 0.0)
        total += mm(jnp.concatenate([high, low], axis=0).astype(bf16), spots, NT)
    want = (total[:group_count] * 128.0 + total[group_count:]).astype(jnp.int32)
    for g in range(group_count):
        want_ref[g] = want[g : g + 1]


def index_lists(order, group_count, leaf_size):
    row_count = order.shape[0]
    assert leaf_size == 256
    return pl.pallas_call(
        index_body,
        out_shape=(
            jax.ShapeDtypeStruct((group_count, 1, row_count // group_count), jnp.int32),
            jax.ShapeDtypeStruct((row_count // leaf_size, 1, leaf_size), jnp.int32),
            jax.ShapeDtypeStruct((row_count // leaf_size, 1, leaf_size), jnp.int32),
            TICK,
        ),
        compiler_params=pltpu.CompilerParams(vmem_limit_bytes=8 * MIB),
        cost_estimate=pl.CostEstimate(flops=2 * 10**9, bytes_accessed=10**5, transcendentals=0),
        name="index_lists",
    )(order.reshape(-1, 128))


def table_body(points_ref, weights_ref, table_ref):
    height = weights_ref.shape[0] + 2 * points_ref.shape[0]
    for h in range(points_ref.shape[1] // 256):
        at = slice(h * 256, (h + 1) * 256)
        high, low = scaled_halves(points_ref[:, at])
        table_ref[h * height : (h + 1) * height, :] = jnp.concatenate(
            [weights_ref[:, at], high, low], axis=0
        ).astype(bf16)


def pick_table(points, weights):
    height = weights.shape[0] + 2 * points.shape[0]
    whole = pl.BlockSpec(memory_space=pltpu.VMEM)
    return pl.pallas_call(
        table_body,
        in_specs=[whole, whole],
        out_specs=whole,
        out_shape=jax.ShapeDtypeStruct((points.shape[1] // 256 * height, 256), bf16),
        compiler_params=pltpu.CompilerParams(vmem_limit_bytes=10 * MIB),
        cost_estimate=pl.CostEstimate(flops=3 * 10**9, bytes_accessed=3 * 10**6, transcendentals=0),
        name="pick_table",
    )(points, weights)


def pick_body(want_ref, table_ref, out_ref):
    group_count, height, pair = out_ref.shape
    high_count = table_ref.shape[0] // height
    batch = 8

    def devices(d, carry):
        want = jnp.concatenate([want_ref[2 * d], want_ref[2 * d + 1]], axis=1)
        low = want & 255
        high = want >> 8
        spots = (lax.broadcasted_iota(jnp.int32, (256, 2 * pair), 0) == low).astype(f32).astype(bf16)
        picked = jnp.zeros((height, 2 * pair), f32)
        for h in range(0, high_count, batch):
            found = mm(table_ref[h * height : (h + batch) * height, :], spots)
            for k in range(batch):
                picked = jnp.where(high == h + k, found[k * height : (k + 1) * height], picked)
        picked = picked.astype(bf16)
        out_ref[2 * d] = picked[:, :pair]
        out_ref[2 * d + 1] = picked[:, pair:]
        return carry

    lax.fori_loop(0, group_count // 2, devices, 0)


def pick(want, table, row_count):
    group_count, _, pair = want.shape
    height = table.shape[0] * 256 // row_count
    whole = pl.BlockSpec(memory_space=pltpu.VMEM)
    return pl.pallas_call(
        pick_body,
        in_specs=[whole, whole],
        out_specs=whole,
        out_shape=jax.ShapeDtypeStruct((group_count, height, pair), bf16),
        compiler_params=pltpu.CompilerParams(vmem_limit_bytes=16 * MIB),
        cost_estimate=pl.CostEstimate(flops=6 * 10**9, bytes_accessed=3 * 10**6, transcendentals=0),
        name="pick",
    )(want, table)


def place_body(src_ref, rank_ref, arrived_ref, leaf_ref, table):
    leaf_count, height, leaf_size = leaf_ref.shape
    pair = arrived_ref.shape[1]
    group_count = arrived_ref.shape[0] // height
    lines = table.shape[0] // height
    pieces = 2 * lines // group_count
    batch = 4
    step = 4
    for g in range(0, group_count, 2):
        two = jnp.concatenate(
            [arrived_ref[(g + k) * height : (g + k + 1) * height, :] for k in range(2)], axis=1
        )
        for k in range(pieces):
            at = (g // 2 * pieces + k) * height
            table[at : at + height, :] = two[:, k * 256 : (k + 1) * 256]

    def leaves(c, carry):
        for n in range(step):
            i = c * step + n
            slot = src_ref[i] * pair + rank_ref[i]
            low = slot & 255
            high = slot >> 8
            spots = (
                lax.broadcasted_iota(jnp.int32, (256, leaf_size), 0) == low
            ).astype(f32).astype(bf16)
            placed = jnp.zeros((height, leaf_size), f32)
            for h in range(0, lines, batch):
                found = mm(table[h * height : (h + batch) * height, :], spots)
                for k in range(batch):
                    placed = jnp.where(high == h + k, found[k * height : (k + 1) * height], placed)
            leaf_ref[i] = placed.astype(bf16)
        return carry

    lax.fori_loop(0, leaf_count // step, leaves, 0)


def place(src, rank, arrived):
    group_count, height, pair = arrived.shape
    leaf_count, _, leaf_size = src.shape
    whole = pl.BlockSpec(memory_space=pltpu.VMEM)
    return pl.pallas_call(
        place_body,
        in_specs=[whole] * 3,
        out_specs=whole,
        out_shape=jax.ShapeDtypeStruct((leaf_count, height, leaf_size), bf16),
        scratch_shapes=[pltpu.VMEM((group_count * pair // 256 * height, 256), bf16)],
        compiler_params=pltpu.CompilerParams(vmem_limit_bytes=14 * MIB),
        cost_estimate=pl.CostEstimate(flops=8 * 10**9, bytes_accessed=2 * 10**6, transcendentals=0),
        name="place",
    )(src, rank, arrived.reshape(group_count * height, pair))


def skeleton_body(leaf_ref, basis_ref, transfer_ref, skel_ref, upper_ref):
    leaf_count, cols, _ = skel_ref.shape

    def cluster(c, carry):
        total = jnp.zeros(upper_ref.shape[1:], f32)
        for n in range(KIDS):
            i = c * KIDS + n
            values = leaf_ref[i, :cols]
            basis_high, basis_low = halves(basis_ref[i])
            skel = mm(values, basis_high) + mm(values, basis_low)
            skel_ref[i] = skel.astype(bf16)
            total += mm3(skel, transfer_ref[i])
        upper_ref[c] = total.astype(bf16)
        return carry

    lax.fori_loop(0, leaf_count // KIDS, cluster, 0)


def skeleton(leaves, basis, transfer):
    leaf_count, _, rank_size = basis.shape
    cols = leaves.shape[1] - 16
    whole = pl.BlockSpec(memory_space=pltpu.VMEM)
    return pl.pallas_call(
        skeleton_body,
        in_specs=[whole] * 3,
        out_specs=(whole, whole),
        out_shape=(
            jax.ShapeDtypeStruct((leaf_count, cols, rank_size), bf16),
            jax.ShapeDtypeStruct((leaf_count // KIDS, cols, rank_size), bf16),
        ),
        compiler_params=pltpu.CompilerParams(vmem_limit_bytes=14 * MIB),
        cost_estimate=pl.CostEstimate(flops=10**9, bytes_accessed=7 * 10**6, transcendentals=0),
        name="skeleton",
    )(leaves, basis, transfer)


def near_body(list_ref, low_ref, own_ref, high_ref, after_ref, out_ref, tick_ref, rows, values):
    tick_ref[...] = jnp.zeros_like(tick_ref)
    leaf_count, height, leaf_size = own_ref.shape
    cols = height - 16
    for part, ref in enumerate((low_ref, own_ref, high_ref)):

        def fill(n, carry, part=part, ref=ref):
            values[part * leaf_count + n] = ref[n, :cols]
            tail = ref[n, cols:].astype(f32)
            rows[part * leaf_count + n] = source_rows(tail[:8], tail[8:])
            return carry

        lax.fori_loop(0, leaf_count, fill, 0)

    def leaf(i, carry):
        tail = own_ref[i, cols:].astype(f32)
        target = target_rows(tail[:8], tail[8:])
        total = jnp.zeros((leaf_size, cols), f32)
        for q in range(list_ref.shape[1]):
            j = list_ref[i, q]
            total += mm(matern(mm(target, rows[j])), values[j], NT)
        out_ref[i] = total
        return carry

    lax.fori_loop(0, leaf_count, leaf, 0)


def near_sums(lists, low, own, high, after):
    leaf_count, near = lists.shape
    height, leaf_size = own.shape[1:]
    cols = height - 16
    whole = pl.BlockSpec(memory_space=pltpu.VMEM)
    pairs = leaf_count * near * leaf_size * leaf_size
    return pl.pallas_call(
        near_body,
        in_specs=[pl.BlockSpec(memory_space=pltpu.SMEM), whole, whole, whole]
        + [pl.BlockSpec(memory_space=pl.ANY)],
        out_specs=(whole, whole),
        out_shape=(jax.ShapeDtypeStruct((leaf_count, leaf_size, cols), f32), TICK),
        scratch_shapes=[
            pltpu.VMEM((3 * leaf_count, AUG, leaf_size), bf16),
            pltpu.VMEM((3 * leaf_count, cols, leaf_size), bf16),
        ],
        compiler_params=pltpu.CompilerParams(vmem_limit_bytes=58 * MIB),
        cost_estimate=pl.CostEstimate(
            flops=pairs * 2500, bytes_accessed=6 * 10**6, transcendentals=2 * pairs
        ),
        name="near_sums",
    )(lists, low, own, high, after)


def fill_rows(points_ref, rows_ref):
    step = 8

    def fill(n, carry):
        for k in range(step):
            rows_ref[n * step + k] = source_rows(*f32_halves(points_ref[n * step + k]))
        return carry

    lax.fori_loop(0, rows_ref.shape[0] // step, fill, 0)


FAR_STEP = 4


def far_body(first, after_count, list_ref, target_ref, points_ref, *refs):
    out_ref, tick_ref, rows_ref = refs[after_count:]

    @pl.when(pl.program_id(0) == 0)
    def _():
        fill_rows(points_ref, rows_ref)

    rank_size = rows_ref.shape[2]
    far = list_ref.shape[1]
    batch = 4
    for n in range(FAR_STEP):
        i = first + pl.program_id(0) * FAR_STEP + n
        target = target_rows(*f32_halves(target_ref[i]))
        for q in range(0, far, batch):
            rows = jnp.concatenate([rows_ref[list_ref[i, q + k]] for k in range(batch)], axis=1)
            out_ref[n, :, q * rank_size : (q + batch) * rank_size] = matern(mm(target, rows))
    tick_ref[...] = jnp.zeros_like(tick_ref)


def far_kernels(first, count, lists, targets, points, *after):
    far = lists.shape[1]
    rank_size = points.shape[2]
    pairs = count * far * rank_size * rank_size
    anywhere = pl.BlockSpec(memory_space=pl.ANY)
    return pl.pallas_call(
        functools.partial(far_body, first, len(after)),
        grid_spec=pltpu.PrefetchScalarGridSpec(
            num_scalar_prefetch=1,
            grid=(count // FAR_STEP,),
            in_specs=[
                pl.BlockSpec(targets.shape, lambda i, s: (0, 0, 0)),
                pl.BlockSpec(points.shape, lambda i, s: (0, 0, 0)),
            ]
            + [anywhere] * len(after),
            out_specs=(
                pl.BlockSpec((FAR_STEP, rank_size, far * rank_size), lambda i, s: (i, 0, 0)),
                pl.BlockSpec(TICK.shape, lambda i, s: (0, 0)),
            ),
            scratch_shapes=[pltpu.VMEM((points.shape[0], AUG, rank_size), bf16)],
        ),
        out_shape=(jax.ShapeDtypeStruct((count, rank_size, far * rank_size), bf16), TICK),
        compiler_params=pltpu.CompilerParams(vmem_limit_bytes=52 * MIB),
        cost_estimate=pl.CostEstimate(
            flops=pairs * 20, bytes_accessed=10**6, transcendentals=0
        ),
        name="far_kernels",
    )(lists, targets, points, *after)


STREAM_STEP = 4


def far_sums_body(
    list_ref, target_ref, points_ref, gathered_ref, stored_ref, after_ref, out_ref, tick_ref, even, odd, stream, rows_ref, weights_ref, sems
):
    tick_ref[...] = jnp.zeros_like(tick_ref)
    early = stored_ref.shape[0]
    late = out_ref.shape[0] - early
    rank_size = weights_ref.shape[2]
    far = list_ref.shape[1]
    batch = 4
    blocks = early // STREAM_STEP
    copies = [
        pltpu.make_async_copy(
            stored_ref.at[pl.ds(k * STREAM_STEP, STREAM_STEP)], stream.at[k % 2], sems.at[k % 2]
        )
        for k in range(blocks)
    ]

    def listed(ref, i, q, n):
        return jnp.concatenate([ref[list_ref[i, q + k]] for k in range(n)], axis=1)

    def fill(i, kernel):
        target = target_rows(*f32_halves(target_ref[i]))
        for q in range(0, far, batch):
            kernel[:, q * rank_size : (q + batch) * rank_size] = matern(
                mm(target, listed(rows_ref, i, q, batch))
            )

    def apply(i, kernel):
        out_ref[i] = mm(kernel, listed(weights_ref, i, 0, far), NT)

    weights_copy = pltpu.make_async_copy(gathered_ref, weights_ref, sems.at[2])
    weights_copy.start()
    for copy in copies[:2]:
        copy.start()
    fill_rows(points_ref, rows_ref)
    fill(early, even)
    weights_copy.wait()

    def two(n, carry):
        i = early + 2 * n
        fill(i + 1, odd)
        apply(i, even[...])
        fill(jnp.minimum(i + 2, early + late - 1), even)
        apply(i + 1, odd[...])
        return carry

    lax.fori_loop(0, late // 2, two, 0)
    for k, copy in enumerate(copies):
        copy.wait()
        for n in range(STREAM_STEP):
            apply(k * STREAM_STEP + n, stream[k % 2, n])
        if k + 2 < blocks:
            copies[k + 2].start()


def far_sums(lists, targets, points, weights, stored, after):
    count, far = lists.shape
    cols, rank_size = weights.shape[1:]
    whole = pl.BlockSpec(memory_space=pltpu.VMEM)
    anywhere = pl.BlockSpec(memory_space=pl.ANY)
    pairs = count * far * rank_size * rank_size
    return pl.pallas_call(
        far_sums_body,
        in_specs=[pl.BlockSpec(memory_space=pltpu.SMEM), whole, whole, anywhere, anywhere, anywhere],
        out_specs=(whole, whole),
        out_shape=(jax.ShapeDtypeStruct((count, rank_size, cols), f32), TICK),
        scratch_shapes=[pltpu.VMEM((rank_size, far * rank_size), bf16)] * 2
        + [
            pltpu.VMEM((2, STREAM_STEP, rank_size, far * rank_size), bf16),
            pltpu.VMEM((points.shape[0], AUG, rank_size), bf16),
            pltpu.VMEM(weights.shape, bf16),
            pltpu.SemaphoreType.DMA((3,)),
        ],
        compiler_params=pltpu.CompilerParams(vmem_limit_bytes=58 * MIB),
        cost_estimate=pl.CostEstimate(
            flops=pairs * 2500, bytes_accessed=24 * 10**6, transcendentals=2 * pairs
        ),
        name="far_sums",
    )(lists, targets, points, weights, stored, after)


def upper_body(list_ref, own_ref, chip_ref, across_ref, after_ref, out_ref):
    dims, rank_size = own_ref.shape[1:]
    cols = out_ref.shape[2]
    batch = 4
    half = chip_ref.shape[0]

    def block_of(place):
        here = chip_ref[jnp.minimum(place, half - 1)]
        there = across_ref[jnp.maximum(place - half, 0)]
        return jnp.where(place < half, here, there)

    for c in range(own_ref.shape[0]):
        target = target_rows(*scaled_halves(own_ref[c]))
        total = jnp.zeros((rank_size, cols), f32)
        for q in range(0, list_ref.shape[1], batch):
            blocks = [block_of(list_ref[c, q + k]) for k in range(batch)]
            values = jnp.concatenate([x[:cols] for x in blocks], axis=1)
            points = jnp.concatenate([x[cols:].astype(f32)[:dims] for x in blocks], axis=1)
            kernel = matern(mm(target, source_rows(*scaled_halves(points))))
            total += mm(kernel, values, NT)
        out_ref[c] = total


def upper_sums(lists, own, chip, across, after):
    count, dims, rank_size = own.shape
    cols = chip.shape[1] - 2 * dims
    whole = pl.BlockSpec(memory_space=pltpu.VMEM)
    pairs = count * lists.shape[1] * rank_size * rank_size
    return pl.pallas_call(
        upper_body,
        in_specs=[pl.BlockSpec(memory_space=pltpu.SMEM), whole, whole, whole]
        + [pl.BlockSpec(memory_space=pl.ANY)],
        out_specs=whole,
        out_shape=jax.ShapeDtypeStruct((count, rank_size, cols), f32),
        compiler_params=pltpu.CompilerParams(vmem_limit_bytes=16 * MIB),
        cost_estimate=pl.CostEstimate(
            flops=pairs * 230, bytes_accessed=8 * 10**6, transcendentals=2 * pairs
        ),
        name="upper_sums",
    )(lists, own, chip, across, after)


def final_body(far_ref, upper_ref, transfer_ref, basis_ref, near_ref, out_ref):
    leaf_count, leaf_size, _ = basis_ref.shape
    step = 4

    def leaves(n, carry):
        upper = upper_ref[n * step // KIDS]
        for k in range(step):
            i = n * step + k
            skeleton = far_ref[i] + mm3(transfer_ref[i], upper)
            potential = mm3(basis_ref[i], skeleton) + near_ref[i]
            at = pl.ds(pl.multiple_of(i * leaf_size, leaf_size), leaf_size)
            out_ref[:, at] = jnp.transpose(potential)
        return carry

    lax.fori_loop(0, leaf_count // step, leaves, 0)


def final(far, upper, transfer, basis, near):
    leaf_count, leaf_size, rank_size = basis.shape
    cols = near.shape[2]
    whole = pl.BlockSpec(memory_space=pltpu.VMEM)
    return pl.pallas_call(
        final_body,
        in_specs=[whole] * 5,
        out_specs=whole,
        out_shape=jax.ShapeDtypeStruct((cols, leaf_count * leaf_size), f32),
        compiler_params=pltpu.CompilerParams(vmem_limit_bytes=20 * MIB),
        cost_estimate=pl.CostEstimate(flops=10**9, bytes_accessed=10**7, transcendentals=0),
        name="final",
    )(far, upper, transfer, basis, near)


def shifted(block, axis, move, count):
    return lax.ppermute(block, axis, [(i, move(i)) for i in range(count)])


def upper_places(clusters, count):
    owner = clusters // count
    group = owner % 16
    bulk = owner // 16
    mine = lax.axis_index("bulk")
    core = (bulk ^ mine) & 1
    hops = (bulk // 2 - mine // 2) & 3
    turn = hops
    return (((core * 4 + turn) * 16) + group) * count + clusters % count


def local(
    points,
    weights,
    leaf_order,
    basis,
    transfer,
    skel_leaf,
    skel_upper,
    near_list,
    leaf_interaction_list,
    far_upper,
):
    row_count = leaf_order.shape[0]
    group_count = lax.axis_size("group")
    bulk_count = lax.axis_size("bulk")
    device_count = group_count * bulk_count
    leaf_count = basis.shape[0]

    want, src, rank, tick = index_lists(leaf_order, group_count, basis.shape[1])
    scaled = skel_leaf.astype(f32) * POINT_SCALE + tick[0]
    subtree_points = lax.all_gather(scaled, "group", axis=0, tiled=True)
    wanted = lax.all_to_all(want, "group", split_axis=0, concat_axis=0, tiled=True)
    picked = pick(wanted, pick_table(points, weights), row_count)
    arrived = lax.all_to_all(picked, "group", split_axis=0, concat_axis=0, tiled=True)

    far_local = leaf_interaction_list - lax.axis_index("bulk") * (group_count * leaf_count)

    own = place(src, rank, arrived)
    skel_wb, upper_wb = skeleton(own, basis, transfer)
    sub_w = lax.all_gather(skel_wb, "group", axis=0, tiled=True)
    forward = [(i, i + 1) for i in range(device_count - 1)]
    backward = [(i + 1, i) for i in range(device_count - 1)]
    low = lax.ppermute(own, ("bulk", "group"), forward)
    high = lax.ppermute(own, ("bulk", "group"), backward)

    def joined(tick, *blocks):
        return jnp.concatenate(blocks, axis=0) + tick[0].astype(bf16)

    mine = jnp.concatenate([upper_wb, skel_upper, jnp.zeros(skel_upper.shape, bf16)], axis=1)
    copies = jnp.tile(mine, (group_count, 1, 1))
    block = lax.all_to_all(copies, "group", split_axis=0, concat_axis=0, tiled=True)
    part = leaf_count // 2
    kernels, tick = far_kernels(0, part, far_local, scaled, subtree_points, copies)
    block = joined(tick, block)
    ring = [shifted(block, "bulk", lambda i, hops=hops: (i - 2 * hops) % bulk_count, bulk_count) for hops in (1, 2, 3)]
    device = lax.axis_index(("bulk", "group"))
    near, tick = near_sums(near_list - (device - 1) * leaf_count, low, own, high, block)
    chip = joined(tick, block, *ring)
    other = shifted(chip, "bulk", lambda i: i ^ 1, bulk_count)
    far, tick = far_sums(far_local, scaled, subtree_points, sub_w, kernels, chip)
    upper = upper_sums(upper_places(far_upper, skel_upper.shape[0]), skel_upper, chip, other, tick)
    return final(far, upper, transfer, basis, near)


def solution(mesh):
    placed = (
        P(None, ("bulk", "group")),
        P(None, ("bulk", "group")),
        P(("bulk", "group")),
        P(("bulk", "group"), None, None),
        P(("bulk", "group"), None, None),
        P(("bulk", "group"), None, None),
        P(("bulk", "group"), None, None),
        P(("bulk", "group"), None),
        P(("bulk", "group"), None),
        P(("bulk", "group"), None),
    )
    return jax.shard_map(
        local, mesh=mesh, in_specs=placed, out_specs=P(None, ("bulk", "group")), check_vma=False
    )
```

profile of v0, /device:TPU:7, one launch (start us, length us, event | category | flops | bytes accessed | tf_op | source)
XLA Modules:
  0.0 203.8 jit_solution(15201115134281236359)
XLA Ops:
  6.5 0.9 copy-done.14
  7.4 3.6 %index_lists.1 = (s32[16,1,384]{2,1,0:T(1,128)}, s32[24,1,256]{2,1,0:T(1,128)S(1)}, s32[24,1,256]{2,1,0:T(1,128)S(1)}, f32[8,128]{1,0:T(8,128)S(1)}) custom-call(s32[48,128]{1,0:T(8,128)S(1)} %bitcast.12), custom_call_target="tpu_custom_call" | custom-call | flops 2000000000 | bytes 100000 | tf_op jit(solution)/shard_map/index_lists/pallas_call | solution.py:129
  11.0 0.7 multiply_add_fusion.target_ref
  11.7 0.0 all-gather.3.cloned.1.call-update
  11.7 7.8 %all-to-all-start = ((s32[16,1,384]{2,1,0:T(1,128)}), s32[16,1,384]{2,1,0:T(1,128)S(1)}, u32[]{:S(2)}, u32[]{:S(2)}) async-start(s32[16,1,384]{2,1,0:T(1,128)} %get-tuple-element.20), calls=%async_computation | async-start | bytes 49152 | tf_op jit(solution)/shard_map/all_to_all | solution.py:601
  19.5 0.0 all-gather.5.cloned.1.call-start
  19.6 0.1 pick_table.1.table_ref
  19.7 6.3 %all-to-all-done.want_ref = s32[16,1,384]{2,1,0:T(1,128)S(1)} async-done(((s32[16,1,384]{2,1,0:T(1,128)}), s32[16,1,384]{2,1,0:T(1,128)S(1)}, u32[]{:S(2)}, u32[]{:S(2)}) %all-to-all-start) | async-done | bytes 24608 | tf_op jit(solution)/shard_map/all_to_all | solution.py:601
  26.0 8.1 %pick.1 = bf16[16,80,384]{2,1,0:T(8,128)(2,1)S(1)} custom-call(s32[16,1,384]{2,1,0:T(1,128)S(1)} %all-to-all-done.want_ref, bf16[1920,256]{1,0:T(8,128)(2,1)S(1)} %pick_table.1.table_ref), custom_call_target="tpu_custom_call" | custom-call | flops 6000000000 | bytes 3000000 | tf_op jit(solution)/shard_map/pick/pallas_call | solution.py:194
  34.0 18.7 %all_to_all.15 = bf16[16,80,384]{2,1,0:T(8,128)(2,1)S(1)} all-to-all(bf16[16,80,384]{2,1,0:T(8,128)(2,1)S(1)} %pick.1), channel_id=1, replica_groups=mesh['bulk'=8,'group'=16] {'group'}, dimensions={0} | all-to-all | bytes 1966080 | tf_op jit(solution)/shard_map/all_to_all | solution.py:603
  52.8 7.6 %place.1.leaf_ref.own_ref = bf16[24,80,256]{2,1,0:T(8,128)(2,1)S(1)} custom-call(s32[24,1,256]{2,1,0:T(1,128)S(1)} %get-tuple-element.18.src_ref, s32[24,1,256]{2,1,0:T(1,128)S(1)} %get-tuple-element.19.rank_ref, bf16[1280,384]{1,0:T(8,128)(2,1)S(1)} %bitcast.11), custom_call_target="tpu_custom_call" | custom-call | flops 8000000000 | bytes 2000000 | tf_op jit(solution)/shard_map/place/pallas_call | solution.py:245
  60.5 0.0 copy-start.10
  60.5 0.0 copy-start.18
  60.5 0.0 copy-start.17
  60.5 2.4 %skeleton.1 = (bf16[24,64,128]{2,1,0:T(8,128)(2,1)S(1)}, bf16[3,64,128]{2,1,0:T(8,128)(2,1)S(1)}) custom-call(bf16[24,80,256]{2,1,0:T(8,128)(2,1)S(1)} %place.1.leaf_ref.own_ref, f32[24,256,128]{2,1,0:T(8,128)S(1)} %copy-done, f32[24,128,128]{2,1,0:T(8,128)S(1)} %copy-done.2), custom_call_target="tpu_custom_call" | custom-call | flops 1000000000 | bytes 7000000 | tf_op jit(solution)/shard_map/skeleton/pallas_call | solution.py:279
  62.9 0.0 copy-done.6
  63.0 0.8 copy-done.8
  63.7 0.0 all-gather.5.cloned.1.call-update
  63.7 0.1 pad.6.clone
  63.8 0.1 maximum_maximum_fusion
  63.9 1.1 tile.4
  65.0 4.3 %all-to-all-start.2 = ((bf16[48,80,128]{2,1,0:T(8,128)(2,1)}), bf16[48,80,128]{2,1,0:T(8,128)(2,1)}, u32[]{:S(2)}, u32[]{:S(2)}) async-start(bf16[48,80,128]{2,1,0:T(8,128)(2,1)} %bitcast.9), calls=%async_computation.2 | async-start | bytes 1966080 | tf_op jit(solution)/shard_map/all_to_all | solution.py:620
  69.3 3.1 %collective-permute-start.3 = (bf16[24,80,256]{2,1,0:T(8,128)(2,1)}, bf16[24,80,256]{2,1,0:T(8,128)(2,1)}, u32[]{:S(2)}, u32[]{:S(2)}) collective-permute-start(bf16[24,80,256]{2,1,0:T(8,128)(2,1)} %copy-done.6), channel_id=1, source_target_pairs={{0,1},{1,2},{2,3},{3,4},{4,5},{5,6},{6,7},{7,8},{8,9},{9,10},{10,1... | collective-permute-start | bytes 2949128 | tf_op jit(solution)/shard_map/ppermute | solution.py:612
  72.4 11.2 %collective-permute-start.4 = (bf16[24,80,256]{2,1,0:T(8,128)(2,1)}, bf16[24,80,256]{2,1,0:T(8,128)(2,1)}, u32[]{:S(2)}, u32[]{:S(2)}) collective-permute-start(bf16[24,80,256]{2,1,0:T(8,128)(2,1)} %copy-done.6), channel_id=1, source_target_pairs={{1,0},{2,1},{3,2},{4,3},{5,4},{6,5},{7,6},{8,7},{9,8},{10,9},{11,1... | collective-permute-start | bytes 2949128 | tf_op jit(solution)/shard_map/ppermute | solution.py:613
  83.6 0.1 copy.13
  83.7 0.6 broadcast_subtract_fusion.list_ref
  84.3 1.2 copy-done.1
  85.6 17.4 %far_kernels.1 = (bf16[12,128,4096]{2,1,0:T(8,128)(2,1)}, f32[8,128]{1,0:T(8,128)S(1)}) custom-call(s32[24,32]{1,0:T(8,128)S(1)} %broadcast_subtract_fusion.1.list_ref, f32[24,8,128]{2,1,0:T(8,128)S(1)} %copy-done.7, f32[384,8,128]{2,1,0:T(8,128)} %all-gather.3.cloned.1.call-done.points_ref, bf16[48,80,128]{2,1,0:T(8,128)(2,1)S(1)} %bitcast.10), custom_call_target="tpu_custom_call" | custom-call | flops 125829120 | bytes 1000000 | tf_op jit(solution)/shard_map/far_kernels/pallas_call | solution.py:382
  102.9 0.0 all-to-all-done.2
  102.9 1.3 broadcast_add_fusion.after_ref
  104.2 0.0 copy-start.15
  104.2 0.3 collective-permute-start.2
  104.5 2.1 %collective-permute-start.1 = (bf16[48,80,128]{2,1,0:T(8,128)(2,1)S(1)}, bf16[48,80,128]{2,1,0:T(8,128)(2,1)}, u32[]{:S(2)}, u32[]{:S(2)}) collective-permute-start(bf16[48,80,128]{2,1,0:T(8,128)(2,1)S(1)} %broadcast_add_fusion.after_ref), channel_id=1, source_target_pairs={{0,64},{16,80},{32,96},{48,112},{64,0},{80,16},{96,32},{112,48},{1... | collective-permute-start | bytes 2949128 | tf_op jit(solution)/shard_map/ppermute | solution.py:566
  106.6 0.0 collective-permute-start
  106.6 7.4 %collective-permute-done.3.low_ref = bf16[24,80,256]{2,1,0:T(8,128)(2,1)} collective-permute-done((bf16[24,80,256]{2,1,0:T(8,128)(2,1)}, bf16[24,80,256]{2,1,0:T(8,128)(2,1)}, u32[]{:S(2)}, u32[]{:S(2)}) %collective-permute-start.3) | collective-permute-done | bytes 983072 | tf_op jit(solution)/shard_map/ppermute | solution.py:612
  114.0 0.0 collective-permute-done.4.high_ref
  114.0 43.0 %near_sums.1 = (f32[24,256,64]{2,1,0:T(8,128)}, f32[8,128]{1,0:T(8,128)}) custom-call(s32[24,12]{1,0:T(8,128)} %broadcast_subtract_fusion.list_ref, bf16[24,80,256]{2,1,0:T(8,128)(2,1)} %collective-permute-done.3.low_ref, bf16[24,80,256]{2,1,0:T(8,128)(2,1)} %copy-done.6, bf16[24,80,256]{2,1,0:T(8,128)(2,1)} %collective-permute-done.4.high_ref, ...), custom_call_target="tpu_custom_call" | custom-call | flops 47185920000 | bytes 6000000 | tf_op jit(solution)/shard_map/near_sums/pallas_call | solution.py:326
  157.0 0.7 convert.7
  157.7 0.0 collective-permute-done.2
  157.7 0.0 collective-permute-done.1
  157.7 0.0 collective-permute-done
  157.7 3.6 %maximum_add_fusion.after_ref.chip_ref = bf16[192,80,128]{2,1,0:T(8,128)(2,1)} fusion(bf16[48,80,128]{2,1,0:T(8,128)(2,1)S(1)} %collective-permute-done.2, bf16[48,80,128]{2,1,0:T(8,128)(2,1)} %collective-permute-done.1, bf16[48,80,128]{2,1,0:T(8,128)(2,1)} %collective-permute-done, bf16[48,80,128]{2,1,0:T(8,128)(2,1)} %copy-done.15, ...), kind=kLoop, calls=%fused_computation | loop fusion | flops 7864320 | bytes 7864576 | tf_op jit(solution)/shard_map/add | solution.py:616
  161.3 0.0 collective-permute-start.5
  161.4 0.0 all-gather.5.cloned.1.call-done.gathered_ref
  161.4 21.8 %far_sums.1 = (f32[24,128,64]{2,1,0:T(8,128)}, f32[8,128]{1,0:T(8,128)}) custom-call(s32[24,32]{1,0:T(8,128)} %copy-done.9, f32[24,8,128]{2,1,0:T(8,128)} %multiply_add_fusion.target_ref, f32[384,8,128]{2,1,0:T(8,128)} %all-gather.3.cloned.1.call-done.points_ref, bf16[384,64,128]{2,1,0:T(8,128)(2,1)} %all-gather.5.cloned.1.call-done.gathered_ref, ...), custom_call_target="tpu_custom_call" | custom-call | flops 31457280000 | bytes 24000000 | tf_op jit(solution)/shard_map/far_sums/pallas_call | solution.py:471
  183.3 0.7 copy-done.11
  183.9 6.9 %upper_sums.1.upper_ref = f32[3,128,64]{2,1,0:T(8,128)S(1)} custom-call(s32[3,32]{1,0:T(4,128)S(1)} %fusion.6.list_ref, bf16[3,8,128]{2,1,0:T(8,128)(2,1)S(1)} %copy-done.10, bf16[192,80,128]{2,1,0:T(8,128)(2,1)} %maximum_add_fusion.after_ref.chip_ref, bf16[192,80,128]{2,1,0:T(8,128)(2,1)} %collective-permute-done.5.across_ref, f32[8,128]{1,0:T(8,128)S(1)} %copy-done.11), custom_call_target="tpu_custom_call" | custom-call | flops 361758720 | bytes 8000000 | tf_op jit(solution)/shard_map/upper_sums/pallas_call | solution.py:519
  190.9 6.1 %final.1 = f32[64,6144]{1,0:T(8,128)} custom-call(f32[24,128,64]{2,1,0:T(8,128)S(1)} %copy-done.5, f32[3,128,64]{2,1,0:T(8,128)S(1)} %upper_sums.1.upper_ref, f32[24,128,128]{2,1,0:T(8,128)S(1)} %copy-done.3, f32[24,256,128]{2,1,0:T(8,128)S(1)} %copy-done, f32[24,256,64]{2,1,0:T(8,128)S(1)} %copy-done.4), custom_call_target="tpu_custom_call" | custom-call | flops 1000000000 | bytes 10000000 | tf_op jit(solution)/shard_map/final/pallas_call | solution.py:554
  (41 shorter events, 0.1 us)
Async XLA Ops:
  6.5 13.0 %copy-start.13 = (f32[8,6144]{1,0:T(8,128)S(1)}, f32[8,6144]{1,0:T(8,128)}, u32[]{:S(2)}) copy-start(f32[8,6144]{1,0:T(8,128)} %points_ref.1) | copy-start | bytes 589828
  6.5 13.0 %copy-start.12 = (f32[64,6144]{1,0:T(8,128)S(1)}, f32[64,6144]{1,0:T(8,128)}, u32[]{:S(2)}) copy-start(f32[64,6144]{1,0:T(8,128)} %weights_ref.1) | copy-start | bytes 4718596
  6.5 77.8 %all-gather.3.cloned.1.call-start = ((), (), s32[]{:S(2)}) async-start(), calls=%async_computation.3 | async-start | bytes 1671168 | tf_op jit(solution)/shard_map/all_gather | solution.py:600
  6.5 0.9 copy-start.14
  7.4 3.6 %copy-start.16 = (bf16[24,8,128]{2,1,0:T(8,128)(2,1)S(1)}, bf16[24,8,128]{2,1,0:T(8,128)(2,1)}, u32[]{:S(2)}) copy-start(bf16[24,8,128]{2,1,0:T(8,128)(2,1)} %param.15) | copy-start | bytes 147460
  11.7 14.2 %all-to-all-start = ((s32[16,1,384]{2,1,0:T(1,128)}), s32[16,1,384]{2,1,0:T(1,128)S(1)}, u32[]{:S(2)}, u32[]{:S(2)}) async-start(s32[16,1,384]{2,1,0:T(1,128)} %get-tuple-element.20), calls=%async_computation | async-start | bytes 49152 | tf_op jit(solution)/shard_map/all_to_all | solution.py:601
  19.5 141.9 %all-gather.5.cloned.1.call-start = ((), (), s32[]{:S(2)}) async-start(), calls=%async_computation.4 | async-start | bytes 6684672 | tf_op jit(solution)/shard_map/all_gather | solution.py:609
  52.8 7.6 %copy-start = (f32[24,256,128]{2,1,0:T(8,128)S(1)}, f32[24,256,128]{2,1,0:T(8,128)}, u32[]{:S(2)}) copy-start(f32[24,256,128]{2,1,0:T(8,128)} %basis_ref.3) | copy-start | bytes 9437188
  52.8 7.7 %copy-start.2 = (f32[24,128,128]{2,1,0:T(8,128)S(1)}, f32[24,128,128]{2,1,0:T(8,128)}, u32[]{:S(2)}) copy-start(f32[24,128,128]{2,1,0:T(8,128)} %transfer_ref.3) | copy-start | bytes 4718596
  60.5 2.5 %copy-start.6 = (bf16[24,80,256]{2,1,0:T(8,128)(2,1)}, bf16[24,80,256]{2,1,0:T(8,128)(2,1)S(1)}, u32[]{:S(2)}) copy-start(bf16[24,80,256]{2,1,0:T(8,128)(2,1)S(1)} %place.1.leaf_ref.own_ref) | copy-start | bytes 2949124
  60.5 3.4 %copy-start.10 = (bf16[3,8,128]{2,1,0:T(8,128)(2,1)S(1)}, bf16[3,8,128]{2,1,0:T(8,128)(2,1)}, u32[]{:S(2)}) copy-start(bf16[3,8,128]{2,1,0:T(8,128)(2,1)} %own_ref.1) | copy-start | bytes 18436
  60.5 23.2 %copy-start.18 = (s32[24,12]{0,1:T(8,128)S(1)}, s32[24,12]{0,1:T(8,128)}, u32[]{:S(2)}) copy-start(s32[24,12]{0,1:T(8,128)} %param.17) | copy-start | bytes 3460
  60.5 23.2 %copy-start.17 = (s32[24,32]{1,0:T(8,128)S(1)}, s32[24,32]{1,0:T(8,128)}, u32[]{:S(2)}) copy-start(s32[24,32]{1,0:T(8,128)} %param.18) | copy-start | bytes 9220
  60.5 23.8 %copy-start.7 = (f32[24,8,128]{2,1,0:T(8,128)S(1)}, f32[24,8,128]{2,1,0:T(8,128)}, u32[]{:S(2)}) copy-start(f32[24,8,128]{2,1,0:T(8,128)} %multiply_add_fusion.target_ref) | copy-start | bytes 294916
  62.9 0.8 copy-start.8
  65.0 38.0 %all-to-all-start.2 = ((bf16[48,80,128]{2,1,0:T(8,128)(2,1)}), bf16[48,80,128]{2,1,0:T(8,128)(2,1)}, u32[]{:S(2)}, u32[]{:S(2)}) async-start(bf16[48,80,128]{2,1,0:T(8,128)(2,1)} %bitcast.9), calls=%async_computation.2 | async-start | bytes 1966080 | tf_op jit(solution)/shard_map/all_to_all | solution.py:620
  69.3 44.7 %collective-permute-start.3 = (bf16[24,80,256]{2,1,0:T(8,128)(2,1)}, bf16[24,80,256]{2,1,0:T(8,128)(2,1)}, u32[]{:S(2)}, u32[]{:S(2)}) collective-permute-start(bf16[24,80,256]{2,1,0:T(8,128)(2,1)} %copy-done.6), channel_id=1, source_target_pairs={{0,1},{1,2},{2,3},{3,4},{4,5},{5,6},{6,7},{7,8},{8,9},{9,10},{10,1... | collective-permute-start | bytes 2949128 | tf_op jit(solution)/shard_map/ppermute | solution.py:612
  72.4 41.6 %collective-permute-start.4 = (bf16[24,80,256]{2,1,0:T(8,128)(2,1)}, bf16[24,80,256]{2,1,0:T(8,128)(2,1)}, u32[]{:S(2)}, u32[]{:S(2)}) collective-permute-start(bf16[24,80,256]{2,1,0:T(8,128)(2,1)} %copy-done.6), channel_id=1, source_target_pairs={{1,0},{2,1},{3,2},{4,3},{5,4},{6,5},{7,6},{8,7},{9,8},{10,9},{11,1... | collective-permute-start | bytes 2949128 | tf_op jit(solution)/shard_map/ppermute | solution.py:613
  83.7 73.3 %copy-start.9 = (s32[24,32]{1,0:T(8,128)}, s32[24,32]{1,0:T(8,128)S(1)}, u32[]{:S(2)}) copy-start(s32[24,32]{1,0:T(8,128)S(1)} %broadcast_subtract_fusion.1.list_ref) | copy-start | bytes 9220
  84.3 1.2 copy-start.1
  104.2 9.8 %copy-start.15 = (bf16[48,80,128]{2,1,0:T(8,128)(2,1)}, bf16[48,80,128]{2,1,0:T(8,128)(2,1)S(1)}, u32[]{:S(2)}) copy-start(bf16[48,80,128]{2,1,0:T(8,128)(2,1)S(1)} %broadcast_add_fusion.after_ref) | copy-start | bytes 2949124
  104.2 53.5 %collective-permute-start.2 = (bf16[48,80,128]{2,1,0:T(8,128)(2,1)S(1)}, bf16[48,80,128]{2,1,0:T(8,128)(2,1)S(1)}, u32[]{:S(2)}, u32[]{:S(2)}) collective-permute-start(bf16[48,80,128]{2,1,0:T(8,128)(2,1)S(1)} %broadcast_add_fusion.after_ref), channel_id=1, source_target_pairs={{0,32},{16,48},{32,64},{48,80},{64,96},{80,112},{96,0},{112,16},{1... | collective-permute-start | bytes 2949128 | tf_op jit(solution)/shard_map/ppermute | solution.py:566
  104.5 53.2 %collective-permute-start.1 = (bf16[48,80,128]{2,1,0:T(8,128)(2,1)S(1)}, bf16[48,80,128]{2,1,0:T(8,128)(2,1)}, u32[]{:S(2)}, u32[]{:S(2)}) collective-permute-start(bf16[48,80,128]{2,1,0:T(8,128)(2,1)S(1)} %broadcast_add_fusion.after_ref), channel_id=1, source_target_pairs={{0,64},{16,80},{32,96},{48,112},{64,0},{80,16},{96,32},{112,48},{1... | collective-permute-start | bytes 2949128 | tf_op jit(solution)/shard_map/ppermute | solution.py:566
  106.6 51.1 %collective-permute-start = (bf16[48,80,128]{2,1,0:T(8,128)(2,1)S(1)}, bf16[48,80,128]{2,1,0:T(8,128)(2,1)}, u32[]{:S(2)}, u32[]{:S(2)}) collective-permute-start(bf16[48,80,128]{2,1,0:T(8,128)(2,1)S(1)} %broadcast_add_fusion.after_ref), channel_id=1, source_target_pairs={{0,96},{16,112},{32,0},{48,16},{64,32},{80,48},{96,64},{112,80},{1... | collective-permute-start | bytes 2949128 | tf_op jit(solution)/shard_map/ppermute | solution.py:566
  157.7 3.6 %copy-start.19 = (s32[3,32]{1,0:T(4,128)S(1)}, s32[3,32]{1,0:T(4,128)}, u32[]{:S(2)}) copy-start(s32[3,32]{1,0:T(4,128)} %param.19) | copy-start | bytes 1156
  161.3 21.9 %collective-permute-start.5 = (bf16[192,80,128]{2,1,0:T(8,128)(2,1)}, bf16[192,80,128]{2,1,0:T(8,128)(2,1)}, u32[]{:S(2)}, u32[]{:S(2)}) collective-permute-start(bf16[192,80,128]{2,1,0:T(8,128)(2,1)} %maximum_add_fusion.after_ref.chip_ref), channel_id=1, source_target_pairs={{0,16},{16,0},{32,48},{48,32},{64,80},{80,64},{96,112},{112,96},{1... | collective-permute-start | bytes 11796488 | tf_op jit(solution)/shard_map/ppermute | solution.py:566
  183.3 0.7 copy-start.11
  183.9 6.9 %copy-start.3 = (f32[24,128,128]{2,1,0:T(8,128)S(1)}, f32[24,128,128]{2,1,0:T(8,128)}, u32[]{:S(2)}) copy-start(f32[24,128,128]{2,1,0:T(8,128)} %transfer_ref.3) | copy-start | bytes 4718596
  183.9 6.9 %copy-start.4 = (f32[24,256,64]{2,1,0:T(8,128)S(1)}, f32[24,256,64]{2,1,0:T(8,128)}, u32[]{:S(2)}) copy-start(f32[24,256,64]{2,1,0:T(8,128)} %get-tuple-element.28.near_ref) | copy-start | bytes 4718596
  183.9 6.9 %copy-start.5 = (f32[24,128,64]{2,1,0:T(8,128)S(1)}, f32[24,128,64]{2,1,0:T(8,128)}, u32[]{:S(2)}) copy-start(f32[24,128,64]{2,1,0:T(8,128)} %get-tuple-element.26.far_ref) | copy-start | bytes 2359300
Sparse Core Ops, SparseCore 0:
  11.8 48.9 all-gather.2
  63.8 86.7 all-gather.4
where the time goes:
time: 204 us
  Pallas kernels  117 us (57%)
  starting transfers between devices  28.9 us (14%)
  blocking collectives  18.7 us (9%)
  waiting for transfers between devices  13.7 us (7%)
  between operations  13.7 us (7%)
  other arithmetic  6.91 us (3%)
  local copies, waits for them, and re-layouts  4.86 us (2%)
    pallas_call x1, Pallas kernels, near_sums(): pl.pallas_call(near_body, in_specs=[pl.BlockSpec(memory_space=pltpu.SMEM)...  43 us
    pallas_call x1, Pallas kernels, far_sums(): pl.pallas_call(far_sums_body, in_specs=[pl.BlockSpec(memory_space=pltpu.S...  21.8 us
    all_to_all x1, blocking collectives, local(): lax.all_to_all(picked, 'group', split_axis=0, concat_axis=0, tiled=True)  18.7 us
    pallas_call x1, Pallas kernels, far_kernels(): pl.pallas_call(functools.partial(far_body, first, len(after)), grid_spec=...  17.4 us
    ppermute x1, starting transfers between devices, local(): high = lax.ppermute(own, ('bulk', 'group'), backward)  11.2 us
    pallas_call x1, Pallas kernels, pick(): pl.pallas_call(pick_body, in_specs=[whole, whole], out_specs=whole, out_s...  8.09 us
    all_to_all x1, starting transfers between devices, local(): lax.all_to_all(want, 'group', split_axis=0, concat_axis=0, tiled=True)  7.78 us
    pallas_call x1, Pallas kernels, place(): pl.pallas_call(place_body, in_specs=[whole] * 3, out_specs=whole, out_sha...  7.63 us
  transfers between devices with their start and end apart: 10, of which 2 were waited for; matrix products, arithmetic and copies ran while one was open for 4% of the time, Pallas kernels for 49%

commit v1 on v0

--- a/solution.py
+++ b/solution.py
@@ -333,7 +333,7 @@
             pltpu.VMEM((3 * leaf_count, AUG, leaf_size), bf16),
             pltpu.VMEM((3 * leaf_count, cols, leaf_size), bf16),
         ],
-        compiler_params=pltpu.CompilerParams(vmem_limit_bytes=58 * MIB),
+        compiler_params=pltpu.CompilerParams(vmem_limit_bytes=16 * MIB),
         cost_estimate=pl.CostEstimate(
             flops=pairs * 2500, bytes_accessed=6 * 10**6, transcendentals=2 * pairs
         ),

time: 204 us -> 203 us (level)
  local copies, waits for them, and re-layouts: 4.86 us -> 7.75 us
  other arithmetic: 6.91 us -> 4.34 us
    unnamed x41 -> x43, local copies, waits for them, and re-layouts: 3.7 us -> 6.58 us
    pallas_call x1, Pallas kernels: 43 us -> 40.9 us  [near_sums(): pl.pallas_call(near_body, in_specs=[pl.BlockSpec(memory_space=pltpu.SMEM)...]
  transfers between devices with their start and end apart: 10 -> 10, of which waited for: 2 -> 2; matrix products, arithmetic and copies ran while one was open for 4% -> 2% of each run, Pallas kernels for 49% -> 49%
where the time goes in v1:
time: 203 us
  Pallas kernels  115 us (57%)
  starting transfers between devices  28.9 us (14%)
  blocking collectives  18.7 us (9%)
  waiting for transfers between devices  14.3 us (7%)
  between operations  13.7 us (7%)
  local copies, waits for them, and re-layouts  7.75 us (4%)
  other arithmetic  4.34 us (2%)
    pallas_call x1, Pallas kernels, near_sums(): pl.pallas_call(near_body, in_specs=[pl.BlockSpec(memory_space=pltpu.SMEM)...  40.9 us
    pallas_call x1, Pallas kernels, far_sums(): pl.pallas_call(far_sums_body, in_specs=[pl.BlockSpec(memory_space=pltpu.S...  21.8 us
    all_to_all x1, blocking collectives, local(): lax.all_to_all(picked, 'group', split_axis=0, concat_axis=0, tiled=True)  18.7 us
    pallas_call x1, Pallas kernels, far_kernels(): pl.pallas_call(functools.partial(far_body, first, len(after)), grid_spec=...  17.4 us
    ppermute x1, starting transfers between devices, local(): high = lax.ppermute(own, ('bulk', 'group'), backward)  11.2 us
    pallas_call x1, Pallas kernels, pick(): pl.pallas_call(pick_body, in_specs=[whole, whole], out_specs=whole, out_s...  8.09 us
    ppermute x1, waiting for transfers between devices, local(): low = lax.ppermute(own, ('bulk', 'group'), forward)  7.93 us
    all_to_all x1, starting transfers between devices, local(): lax.all_to_all(want, 'group', split_axis=0, concat_axis=0, tiled=True)  7.78 us
  transfers between devices with their start and end apart: 10, of which 2 were waited for; matrix products, arithmetic and copies ran while one was open for 2% of the time, Pallas kernels for 49%

profile of v1, /device:TPU:7, one launch (start us, length us, event | category | flops | bytes accessed | tf_op | source)
XLA Modules:
  0.0 202.7 jit_solution(18383359349317807426)
XLA Ops:
  6.5 0.9 copy-done.16
  7.4 3.6 %index_lists.1 = (s32[16,1,384]{2,1,0:T(1,128)}, s32[24,1,256]{2,1,0:T(1,128)S(1)}, s32[24,1,256]{2,1,0:T(1,128)S(1)}, f32[8,128]{1,0:T(8,128)S(1)}) custom-call(s32[48,128]{1,0:T(8,128)S(1)} %bitcast.12), custom_call_target="tpu_custom_call" | custom-call | flops 2000000000 | bytes 100000 | tf_op jit(solution)/shard_map/index_lists/pallas_call | solution.py:129
  11.0 0.7 multiply_add_fusion.target_ref
  11.7 0.0 all-gather.3.cloned.1.call-update
  11.7 7.8 %all-to-all-start = ((s32[16,1,384]{2,1,0:T(1,128)}), s32[16,1,384]{2,1,0:T(1,128)S(1)}, u32[]{:S(2)}, u32[]{:S(2)}) async-start(s32[16,1,384]{2,1,0:T(1,128)} %get-tuple-element.20), calls=%async_computation | async-start | bytes 49152 | tf_op jit(solution)/shard_map/all_to_all | solution.py:601
  19.5 0.0 all-gather.5.cloned.1.call-start
  19.6 0.1 pick_table.1.table_ref
  19.7 6.3 %all-to-all-done.want_ref = s32[16,1,384]{2,1,0:T(1,128)S(1)} async-done(((s32[16,1,384]{2,1,0:T(1,128)}), s32[16,1,384]{2,1,0:T(1,128)S(1)}, u32[]{:S(2)}, u32[]{:S(2)}) %all-to-all-start) | async-done | bytes 24608 | tf_op jit(solution)/shard_map/all_to_all | solution.py:601
  26.0 8.1 %pick.1 = bf16[16,80,384]{2,1,0:T(8,128)(2,1)S(1)} custom-call(s32[16,1,384]{2,1,0:T(1,128)S(1)} %all-to-all-done.want_ref, bf16[1920,256]{1,0:T(8,128)(2,1)S(1)} %pick_table.1.table_ref), custom_call_target="tpu_custom_call" | custom-call | flops 6000000000 | bytes 3000000 | tf_op jit(solution)/shard_map/pick/pallas_call | solution.py:194
  34.0 18.7 %all_to_all.15 = bf16[16,80,384]{2,1,0:T(8,128)(2,1)S(1)} all-to-all(bf16[16,80,384]{2,1,0:T(8,128)(2,1)S(1)} %pick.1), channel_id=1, replica_groups=mesh['bulk'=8,'group'=16] {'group'}, dimensions={0} | all-to-all | bytes 1966080 | tf_op jit(solution)/shard_map/all_to_all | solution.py:603
  52.8 7.6 %place.1.leaf_ref.own_ref = bf16[24,80,256]{2,1,0:T(8,128)(2,1)S(1)} custom-call(s32[24,1,256]{2,1,0:T(1,128)S(1)} %get-tuple-element.18.src_ref, s32[24,1,256]{2,1,0:T(1,128)S(1)} %get-tuple-element.19.rank_ref, bf16[1280,384]{1,0:T(8,128)(2,1)S(1)} %bitcast.11), custom_call_target="tpu_custom_call" | custom-call | flops 8000000000 | bytes 2000000 | tf_op jit(solution)/shard_map/place/pallas_call | solution.py:245
  60.4 0.0 copy-start.12
  60.4 0.0 copy-start.19
  60.5 0.0 copy-start.18
  60.5 2.4 %skeleton.1 = (bf16[24,64,128]{2,1,0:T(8,128)(2,1)S(1)}, bf16[3,64,128]{2,1,0:T(8,128)(2,1)S(1)}) custom-call(bf16[24,80,256]{2,1,0:T(8,128)(2,1)S(1)} %place.1.leaf_ref.own_ref, f32[24,256,128]{2,1,0:T(8,128)S(1)} %copy-done, f32[24,128,128]{2,1,0:T(8,128)S(1)} %copy-done.2), custom_call_target="tpu_custom_call" | custom-call | flops 1000000000 | bytes 7000000 | tf_op jit(solution)/shard_map/skeleton/pallas_call | solution.py:279
  62.9 0.0 copy-done.7
  62.9 0.7 copy-done.10
  63.7 0.0 all-gather.5.cloned.1.call-update
  63.7 0.1 pad.6.clone
  63.8 0.1 maximum_maximum_fusion
  63.9 1.1 tile.4
  64.9 4.3 %all-to-all-start.2 = ((bf16[48,80,128]{2,1,0:T(8,128)(2,1)}), bf16[48,80,128]{2,1,0:T(8,128)(2,1)}, u32[]{:S(2)}, u32[]{:S(2)}) async-start(bf16[48,80,128]{2,1,0:T(8,128)(2,1)} %bitcast.9), calls=%async_computation.2 | async-start | bytes 1966080 | tf_op jit(solution)/shard_map/all_to_all | solution.py:620
  69.3 3.1 %collective-permute-start.3 = (bf16[24,80,256]{2,1,0:T(8,128)(2,1)}, bf16[24,80,256]{2,1,0:T(8,128)(2,1)}, u32[]{:S(2)}, u32[]{:S(2)}) collective-permute-start(bf16[24,80,256]{2,1,0:T(8,128)(2,1)} %copy-done.7), channel_id=1, source_target_pairs={{0,1},{1,2},{2,3},{3,4},{4,5},{5,6},{6,7},{7,8},{8,9},{9,10},{10,1... | collective-permute-start | bytes 2949128 | tf_op jit(solution)/shard_map/ppermute | solution.py:612
  72.4 11.2 %collective-permute-start.4 = (bf16[24,80,256]{2,1,0:T(8,128)(2,1)}, bf16[24,80,256]{2,1,0:T(8,128)(2,1)}, u32[]{:S(2)}, u32[]{:S(2)}) collective-permute-start(bf16[24,80,256]{2,1,0:T(8,128)(2,1)} %copy-done.7), channel_id=1, source_target_pairs={{1,0},{2,1},{3,2},{4,3},{5,4},{6,5},{7,6},{8,7},{9,8},{10,9},{11,1... | collective-permute-start | bytes 2949128 | tf_op jit(solution)/shard_map/ppermute | solution.py:613
  83.6 0.1 copy.13
  83.7 0.0 all-gather.3.cloned.1.call-done.points_ref
  83.8 0.0 copy-start.1
  83.8 1.2 copy-done.1
  85.0 17.4 %far_kernels.1 = (bf16[12,128,4096]{2,1,0:T(8,128)(2,1)}, f32[8,128]{1,0:T(8,128)S(1)}) custom-call(s32[24,32]{1,0:T(8,128)S(1)} %broadcast_subtract_fusion.1.list_ref, f32[24,8,128]{2,1,0:T(8,128)S(1)} %copy-done.9, f32[384,8,128]{2,1,0:T(8,128)} %all-gather.3.cloned.1.call-done.points_ref, bf16[48,80,128]{2,1,0:T(8,128)(2,1)S(1)} %bitcast.10), custom_call_target="tpu_custom_call" | custom-call | flops 125829120 | bytes 1000000 | tf_op jit(solution)/shard_map/far_kernels/pallas_call | solution.py:382
  102.4 0.0 all-to-all-done.2
  102.4 1.3 broadcast_add_fusion.after_ref
  103.6 0.3 collective-permute-start.2
  103.9 2.1 %collective-permute-start.1 = (bf16[48,80,128]{2,1,0:T(8,128)(2,1)S(1)}, bf16[48,80,128]{2,1,0:T(8,128)(2,1)S(1)}, u32[]{:S(2)}, u32[]{:S(2)}) collective-permute-start(bf16[48,80,128]{2,1,0:T(8,128)(2,1)S(1)} %broadcast_add_fusion.after_ref), channel_id=1, source_target_pairs={{0,64},{16,80},{32,96},{48,112},{64,0},{80,16},{96,32},{112,48},{1... | collective-permute-start | bytes 2949128 | tf_op jit(solution)/shard_map/ppermute | solution.py:566
  106.1 0.0 collective-permute-start
  106.1 7.9 %collective-permute-done.3.low_ref = bf16[24,80,256]{2,1,0:T(8,128)(2,1)} collective-permute-done((bf16[24,80,256]{2,1,0:T(8,128)(2,1)}, bf16[24,80,256]{2,1,0:T(8,128)(2,1)}, u32[]{:S(2)}, u32[]{:S(2)}) %collective-permute-start.3) | collective-permute-done | bytes 983072 | tf_op jit(solution)/shard_map/ppermute | solution.py:612
  114.0 0.0 collective-permute-done.4.high_ref
  114.0 1.2 copy-done.8
  115.2 40.9 %near_sums.1 = (f32[24,256,64]{2,1,0:T(8,128)S(1)}, f32[8,128]{1,0:T(8,128)S(1)}) custom-call(s32[24,12]{1,0:T(8,128)S(1)} %broadcast_subtract_fusion.list_ref, bf16[24,80,256]{2,1,0:T(8,128)(2,1)} %collective-permute-done.3.low_ref, bf16[24,80,256]{2,1,0:T(8,128)(2,1)S(1)} %copy-done.8, bf16[24,80,256]{2,1,0:T(8,128)(2,1)} %collective-permute-done.4.high_ref, ...), custom_call_target="tpu_custom_call" | custom-call | flops 47185920000 | bytes 6000000 | tf_op jit(solution)/shard_map/near_sums/pallas_call | solution.py:326
  156.2 1.7 copy-done.4
  157.9 0.0 collective-permute-done.2
  157.9 0.0 collective-permute-done.1
  158.0 2.3 %maximum_add_fusion.after_ref.chip_ref = bf16[192,80,128]{2,1,0:T(8,128)(2,1)} fusion(bf16[48,80,128]{2,1,0:T(8,128)(2,1)S(1)} %collective-permute-done.2, bf16[48,80,128]{2,1,0:T(8,128)(2,1)S(1)} %collective-permute-done.1, bf16[48,80,128]{2,1,0:T(8,128)(2,1)S(1)} %collective-permute-done, bf16[48,80,128]{2,1,0:T(8,128)(2,1)S(1)} %broadcast_add_fusion.after_ref, ...), kind=kLoop, calls=%fused_computation | loop fusion | flops 7864320 | bytes 7864576 | tf_op jit(solution)/shard_map/add | solution.py:616
  160.2 0.0 collective-permute-start.5
  160.3 0.0 all-gather.5.cloned.1.call-done.gathered_ref
  160.3 21.8 %far_sums.1 = (f32[24,128,64]{2,1,0:T(8,128)}, f32[8,128]{1,0:T(8,128)}) custom-call(s32[24,32]{1,0:T(8,128)} %copy-done.11, f32[24,8,128]{2,1,0:T(8,128)} %multiply_add_fusion.target_ref, f32[384,8,128]{2,1,0:T(8,128)} %all-gather.3.cloned.1.call-done.points_ref, bf16[384,64,128]{2,1,0:T(8,128)(2,1)} %all-gather.5.cloned.1.call-done.gathered_ref, ...), custom_call_target="tpu_custom_call" | custom-call | flops 31457280000 | bytes 24000000 | tf_op jit(solution)/shard_map/far_sums/pallas_call | solution.py:471
  182.1 0.7 copy-done.13
  182.8 6.9 %upper_sums.1.upper_ref = f32[3,128,64]{2,1,0:T(8,128)S(1)} custom-call(s32[3,32]{1,0:T(4,128)S(1)} %fusion.6.list_ref, bf16[3,8,128]{2,1,0:T(8,128)(2,1)S(1)} %copy-done.12, bf16[192,80,128]{2,1,0:T(8,128)(2,1)} %maximum_add_fusion.after_ref.chip_ref, bf16[192,80,128]{2,1,0:T(8,128)(2,1)} %collective-permute-done.5.across_ref, f32[8,128]{1,0:T(8,128)S(1)} %copy-done.13), custom_call_target="tpu_custom_call" | custom-call | flops 361758720 | bytes 8000000 | tf_op jit(solution)/shard_map/upper_sums/pallas_call | solution.py:519
  189.7 6.1 %final.1 = f32[64,6144]{1,0:T(8,128)} custom-call(f32[24,128,64]{2,1,0:T(8,128)S(1)} %copy-done.6, f32[3,128,64]{2,1,0:T(8,128)S(1)} %upper_sums.1.upper_ref, f32[24,128,128]{2,1,0:T(8,128)S(1)} %copy-done.3, f32[24,256,128]{2,1,0:T(8,128)S(1)} %copy-done, f32[24,256,64]{2,1,0:T(8,128)S(1)} %copy-done.5), custom_call_target="tpu_custom_call" | custom-call | flops 1000000000 | bytes 10000000 | tf_op jit(solution)/shard_map/final/pallas_call | solution.py:554
  (43 shorter events, 0.1 us)
Async XLA Ops:
  6.5 13.0 %copy-start.15 = (f32[8,6144]{1,0:T(8,128)S(1)}, f32[8,6144]{1,0:T(8,128)}, u32[]{:S(2)}) copy-start(f32[8,6144]{1,0:T(8,128)} %points_ref.1) | copy-start | bytes 589828
  6.5 13.0 %copy-start.14 = (f32[64,6144]{1,0:T(8,128)S(1)}, f32[64,6144]{1,0:T(8,128)}, u32[]{:S(2)}) copy-start(f32[64,6144]{1,0:T(8,128)} %weights_ref.1) | copy-start | bytes 4718596
  6.5 77.2 %all-gather.3.cloned.1.call-start = ((), (), s32[]{:S(2)}) async-start(), calls=%async_computation.3 | async-start | bytes 1671168 | tf_op jit(solution)/shard_map/all_gather | solution.py:600
  6.5 0.9 copy-start.16
  7.4 3.6 %copy-start.17 = (bf16[24,8,128]{2,1,0:T(8,128)(2,1)S(1)}, bf16[24,8,128]{2,1,0:T(8,128)(2,1)}, u32[]{:S(2)}) copy-start(bf16[24,8,128]{2,1,0:T(8,128)(2,1)} %param.15) | copy-start | bytes 147460
  11.7 14.2 %all-to-all-start = ((s32[16,1,384]{2,1,0:T(1,128)}), s32[16,1,384]{2,1,0:T(1,128)S(1)}, u32[]{:S(2)}, u32[]{:S(2)}) async-start(s32[16,1,384]{2,1,0:T(1,128)} %get-tuple-element.20), calls=%async_computation | async-start | bytes 49152 | tf_op jit(solution)/shard_map/all_to_all | solution.py:601
  19.5 140.8 %all-gather.5.cloned.1.call-start = ((), (), s32[]{:S(2)}) async-start(), calls=%async_computation.4 | async-start | bytes 6684672 | tf_op jit(solution)/shard_map/all_gather | solution.py:609
  52.8 7.6 %copy-start = (f32[24,256,128]{2,1,0:T(8,128)S(1)}, f32[24,256,128]{2,1,0:T(8,128)}, u32[]{:S(2)}) copy-start(f32[24,256,128]{2,1,0:T(8,128)} %basis_ref.3) | copy-start | bytes 9437188
  52.8 7.7 %copy-start.2 = (f32[24,128,128]{2,1,0:T(8,128)S(1)}, f32[24,128,128]{2,1,0:T(8,128)}, u32[]{:S(2)}) copy-start(f32[24,128,128]{2,1,0:T(8,128)} %transfer_ref.3) | copy-start | bytes 4718596
  60.4 2.5 %copy-start.7 = (bf16[24,80,256]{2,1,0:T(8,128)(2,1)}, bf16[24,80,256]{2,1,0:T(8,128)(2,1)S(1)}, u32[]{:S(2)}) copy-start(bf16[24,80,256]{2,1,0:T(8,128)(2,1)S(1)} %place.1.leaf_ref.own_ref) | copy-start | bytes 2949124
  60.4 3.3 %copy-start.12 = (bf16[3,8,128]{2,1,0:T(8,128)(2,1)S(1)}, bf16[3,8,128]{2,1,0:T(8,128)(2,1)}, u32[]{:S(2)}) copy-start(bf16[3,8,128]{2,1,0:T(8,128)(2,1)} %own_ref.1) | copy-start | bytes 18436
  60.4 23.2 %copy-start.19 = (s32[24,12]{0,1:T(8,128)S(1)}, s32[24,12]{0,1:T(8,128)}, u32[]{:S(2)}) copy-start(s32[24,12]{0,1:T(8,128)} %param.17) | copy-start | bytes 3460
  60.5 23.3 %copy-start.18 = (s32[24,32]{1,0:T(8,128)S(1)}, s32[24,32]{1,0:T(8,128)}, u32[]{:S(2)}) copy-start(s32[24,32]{1,0:T(8,128)} %param.18) | copy-start | bytes 9220
  60.5 23.3 %copy-start.9 = (f32[24,8,128]{2,1,0:T(8,128)S(1)}, f32[24,8,128]{2,1,0:T(8,128)}, u32[]{:S(2)}) copy-start(f32[24,8,128]{2,1,0:T(8,128)} %multiply_add_fusion.target_ref) | copy-start | bytes 294916
  62.9 0.7 copy-start.10
  64.9 37.4 %all-to-all-start.2 = ((bf16[48,80,128]{2,1,0:T(8,128)(2,1)}), bf16[48,80,128]{2,1,0:T(8,128)(2,1)}, u32[]{:S(2)}, u32[]{:S(2)}) async-start(bf16[48,80,128]{2,1,0:T(8,128)(2,1)} %bitcast.9), calls=%async_computation.2 | async-start | bytes 1966080 | tf_op jit(solution)/shard_map/all_to_all | solution.py:620
  69.3 44.7 %collective-permute-start.3 = (bf16[24,80,256]{2,1,0:T(8,128)(2,1)}, bf16[24,80,256]{2,1,0:T(8,128)(2,1)}, u32[]{:S(2)}, u32[]{:S(2)}) collective-permute-start(bf16[24,80,256]{2,1,0:T(8,128)(2,1)} %copy-done.7), channel_id=1, source_target_pairs={{0,1},{1,2},{2,3},{3,4},{4,5},{5,6},{6,7},{7,8},{8,9},{9,10},{10,1... | collective-permute-start | bytes 2949128 | tf_op jit(solution)/shard_map/ppermute | solution.py:612
  72.4 41.6 %collective-permute-start.4 = (bf16[24,80,256]{2,1,0:T(8,128)(2,1)}, bf16[24,80,256]{2,1,0:T(8,128)(2,1)}, u32[]{:S(2)}, u32[]{:S(2)}) collective-permute-start(bf16[24,80,256]{2,1,0:T(8,128)(2,1)} %copy-done.7), channel_id=1, source_target_pairs={{1,0},{2,1},{3,2},{4,3},{5,4},{6,5},{7,6},{8,7},{9,8},{10,9},{11,1... | collective-permute-start | bytes 2949128 | tf_op jit(solution)/shard_map/ppermute | solution.py:613
  83.7 72.4 %copy-start.11 = (s32[24,32]{1,0:T(8,128)}, s32[24,32]{1,0:T(8,128)S(1)}, u32[]{:S(2)}) copy-start(s32[24,32]{1,0:T(8,128)S(1)} %broadcast_subtract_fusion.1.list_ref) | copy-start | bytes 9220
  83.8 1.2 copy-start.1
  103.6 54.3 %collective-permute-start.2 = (bf16[48,80,128]{2,1,0:T(8,128)(2,1)S(1)}, bf16[48,80,128]{2,1,0:T(8,128)(2,1)S(1)}, u32[]{:S(2)}, u32[]{:S(2)}) collective-permute-start(bf16[48,80,128]{2,1,0:T(8,128)(2,1)S(1)} %broadcast_add_fusion.after_ref), channel_id=1, source_target_pairs={{0,32},{16,48},{32,64},{48,80},{64,96},{80,112},{96,0},{112,16},{1... | collective-permute-start | bytes 2949128 | tf_op jit(solution)/shard_map/ppermute | solution.py:566
  103.9 54.0 %collective-permute-start.1 = (bf16[48,80,128]{2,1,0:T(8,128)(2,1)S(1)}, bf16[48,80,128]{2,1,0:T(8,128)(2,1)S(1)}, u32[]{:S(2)}, u32[]{:S(2)}) collective-permute-start(bf16[48,80,128]{2,1,0:T(8,128)(2,1)S(1)} %broadcast_add_fusion.after_ref), channel_id=1, source_target_pairs={{0,64},{16,80},{32,96},{48,112},{64,0},{80,16},{96,32},{112,48},{1... | collective-permute-start | bytes 2949128 | tf_op jit(solution)/shard_map/ppermute | solution.py:566
  106.1 51.9 %collective-permute-start = (bf16[48,80,128]{2,1,0:T(8,128)(2,1)S(1)}, bf16[48,80,128]{2,1,0:T(8,128)(2,1)S(1)}, u32[]{:S(2)}, u32[]{:S(2)}) collective-permute-start(bf16[48,80,128]{2,1,0:T(8,128)(2,1)S(1)} %broadcast_add_fusion.after_ref), channel_id=1, source_target_pairs={{0,96},{16,112},{32,0},{48,16},{64,32},{80,48},{96,64},{112,80},{1... | collective-permute-start | bytes 2949128 | tf_op jit(solution)/shard_map/ppermute | solution.py:566
  114.0 1.2 copy-start.8
  156.2 1.8 copy-start.4
  157.9 2.3 %copy-start.20 = (s32[3,32]{1,0:T(4,128)S(1)}, s32[3,32]{1,0:T(4,128)}, u32[]{:S(2)}) copy-start(s32[3,32]{1,0:T(4,128)} %param.19) | copy-start | bytes 1156
  160.2 21.9 %collective-permute-start.5 = (bf16[192,80,128]{2,1,0:T(8,128)(2,1)}, bf16[192,80,128]{2,1,0:T(8,128)(2,1)}, u32[]{:S(2)}, u32[]{:S(2)}) collective-permute-start(bf16[192,80,128]{2,1,0:T(8,128)(2,1)} %maximum_add_fusion.after_ref.chip_ref), channel_id=1, source_target_pairs={{0,16},{16,0},{32,48},{48,32},{64,80},{80,64},{96,112},{112,96},{1... | collective-permute-start | bytes 11796488 | tf_op jit(solution)/shard_map/ppermute | solution.py:566
  182.1 0.7 copy-start.13
  182.8 6.9 %copy-start.3 = (f32[24,128,128]{2,1,0:T(8,128)S(1)}, f32[24,128,128]{2,1,0:T(8,128)}, u32[]{:S(2)}) copy-start(f32[24,128,128]{2,1,0:T(8,128)} %transfer_ref.3) | copy-start | bytes 4718596
  182.8 6.9 %copy-start.5 = (f32[24,256,64]{2,1,0:T(8,128)S(1)}, f32[24,256,64]{2,1,0:T(8,128)}, u32[]{:S(2)}) copy-start(f32[24,256,64]{2,1,0:T(8,128)} %copy-done.4) | copy-start | bytes 4718596
  182.8 6.9 %copy-start.6 = (f32[24,128,64]{2,1,0:T(8,128)S(1)}, f32[24,128,64]{2,1,0:T(8,128)}, u32[]{:S(2)}) copy-start(f32[24,128,64]{2,1,0:T(8,128)} %get-tuple-element.26.far_ref) | copy-start | bytes 2359300
Sparse Core Ops, SparseCore 0:
  11.8 48.9 all-gather.2
  63.8 86.8 all-gather.4

commit v2 on v1

--- a/solution.py
+++ b/solution.py
@@ -314,7 +314,12 @@
         out_ref[i] = total
         return carry
 
-    lax.fori_loop(0, leaf_count, leaf, 0)
+    def leaves(n, carry):
+        for k in range(4):
+            leaf(4 * n + k, carry)
+        return carry
+
+    lax.fori_loop(0, leaf_count // 4, leaves, 0)
 
 
 def near_sums(lists, low, own, high, after):

time: 203 us -> 197 us (0.970)
  Pallas kernels: 115 us -> 109 us
    pallas_call x1, Pallas kernels: 40.9 us -> 34.8 us  [near_sums(): pl.pallas_call(near_body, in_specs=[pl.BlockSpec(memory_space=pltpu.SMEM)...]
  transfers between devices with their start and end apart: 10 -> 10, of which waited for: 2 -> 2; matrix products, arithmetic and copies ran while one was open for 2% -> 3% of each run, Pallas kernels for 49% -> 47%
where the time goes in v2:
time: 197 us
  Pallas kernels  109 us (55%)
  starting transfers between devices  28.9 us (15%)
  blocking collectives  18.7 us (9%)
  waiting for transfers between devices  14.3 us (7%)
  between operations  13.7 us (7%)
  local copies, waits for them, and re-layouts  7.75 us (4%)
  other arithmetic  4.34 us (2%)
    pallas_call x1, Pallas kernels, near_sums(): pl.pallas_call(near_body, in_specs=[pl.BlockSpec(memory_space=pltpu.SMEM)...  34.8 us
    pallas_call x1, Pallas kernels, far_sums(): pl.pallas_call(far_sums_body, in_specs=[pl.BlockSpec(memory_space=pltpu.S...  21.8 us
    all_to_all x1, blocking collectives, local(): lax.all_to_all(picked, 'group', split_axis=0, concat_axis=0, tiled=True)  18.7 us
    pallas_call x1, Pallas kernels, far_kernels(): pl.pallas_call(functools.partial(far_body, first, len(after)), grid_spec=...  17.4 us
    ppermute x1, starting transfers between devices, local(): high = lax.ppermute(own, ('bulk', 'group'), backward)  11.2 us
    pallas_call x1, Pallas kernels, pick(): pl.pallas_call(pick_body, in_specs=[whole, whole], out_specs=whole, out_s...  8.09 us
    ppermute x1, waiting for transfers between devices, local(): low = lax.ppermute(own, ('bulk', 'group'), forward)  7.93 us
    all_to_all x1, starting transfers between devices, local(): lax.all_to_all(want, 'group', split_axis=0, concat_axis=0, tiled=True)  7.78 us
  transfers between devices with their start and end apart: 10, of which 2 were waited for; matrix products, arithmetic and copies ran while one was open for 3% of the time, Pallas kernels for 47%

profile of v2, /device:TPU:7, one launch (start us, length us, event | category | flops | bytes accessed | tf_op | source)
XLA Modules:
  0.0 196.5 jit_solution(11519345137206002680)
XLA Ops:
  6.5 0.9 copy-done.16
  7.4 3.6 %index_lists.1 = (s32[16,1,384]{2,1,0:T(1,128)}, s32[24,1,256]{2,1,0:T(1,128)S(1)}, s32[24,1,256]{2,1,0:T(1,128)S(1)}, f32[8,128]{1,0:T(8,128)S(1)}) custom-call(s32[48,128]{1,0:T(8,128)S(1)} %bitcast.12), custom_call_target="tpu_custom_call" | custom-call | flops 2000000000 | bytes 100000 | tf_op jit(solution)/shard_map/index_lists/pallas_call | solution.py:129
  11.0 0.7 multiply_add_fusion.target_ref
  11.7 0.0 all-gather.3.cloned.1.call-update
  11.7 7.8 %all-to-all-start = ((s32[16,1,384]{2,1,0:T(1,128)}), s32[16,1,384]{2,1,0:T(1,128)S(1)}, u32[]{:S(2)}, u32[]{:S(2)}) async-start(s32[16,1,384]{2,1,0:T(1,128)} %get-tuple-element.20), calls=%async_computation | async-start | bytes 49152 | tf_op jit(solution)/shard_map/all_to_all | solution.py:606
  19.5 0.0 all-gather.5.cloned.1.call-start
  19.6 0.1 pick_table.1.table_ref
  19.7 6.3 %all-to-all-done.want_ref = s32[16,1,384]{2,1,0:T(1,128)S(1)} async-done(((s32[16,1,384]{2,1,0:T(1,128)}), s32[16,1,384]{2,1,0:T(1,128)S(1)}, u32[]{:S(2)}, u32[]{:S(2)}) %all-to-all-start) | async-done | bytes 24608 | tf_op jit(solution)/shard_map/all_to_all | solution.py:606
  26.0 8.1 %pick.1 = bf16[16,80,384]{2,1,0:T(8,128)(2,1)S(1)} custom-call(s32[16,1,384]{2,1,0:T(1,128)S(1)} %all-to-all-done.want_ref, bf16[1920,256]{1,0:T(8,128)(2,1)S(1)} %pick_table.1.table_ref), custom_call_target="tpu_custom_call" | custom-call | flops 6000000000 | bytes 3000000 | tf_op jit(solution)/shard_map/pick/pallas_call | solution.py:194
  34.0 18.7 %all_to_all.15 = bf16[16,80,384]{2,1,0:T(8,128)(2,1)S(1)} all-to-all(bf16[16,80,384]{2,1,0:T(8,128)(2,1)S(1)} %pick.1), channel_id=1, replica_groups=mesh['bulk'=8,'group'=16] {'group'}, dimensions={0} | all-to-all | bytes 1966080 | tf_op jit(solution)/shard_map/all_to_all | solution.py:608
  52.8 7.6 %place.1.leaf_ref.own_ref = bf16[24,80,256]{2,1,0:T(8,128)(2,1)S(1)} custom-call(s32[24,1,256]{2,1,0:T(1,128)S(1)} %get-tuple-element.18.src_ref, s32[24,1,256]{2,1,0:T(1,128)S(1)} %get-tuple-element.19.rank_ref, bf16[1280,384]{1,0:T(8,128)(2,1)S(1)} %bitcast.11), custom_call_target="tpu_custom_call" | custom-call | flops 8000000000 | bytes 2000000 | tf_op jit(solution)/shard_map/place/pallas_call | solution.py:245
  60.4 0.0 copy-start.12
  60.4 0.0 copy-start.19
  60.5 0.0 copy-start.18
  60.5 2.4 %skeleton.1 = (bf16[24,64,128]{2,1,0:T(8,128)(2,1)S(1)}, bf16[3,64,128]{2,1,0:T(8,128)(2,1)S(1)}) custom-call(bf16[24,80,256]{2,1,0:T(8,128)(2,1)S(1)} %place.1.leaf_ref.own_ref, f32[24,256,128]{2,1,0:T(8,128)S(1)} %copy-done, f32[24,128,128]{2,1,0:T(8,128)S(1)} %copy-done.2), custom_call_target="tpu_custom_call" | custom-call | flops 1000000000 | bytes 7000000 | tf_op jit(solution)/shard_map/skeleton/pallas_call | solution.py:279
  62.9 0.0 copy-done.7
  62.9 0.7 copy-done.10
  63.7 0.0 all-gather.5.cloned.1.call-update
  63.7 0.1 pad.6.clone
  63.8 0.1 maximum_maximum_fusion
  63.9 1.1 tile.4
  64.9 4.3 %all-to-all-start.2 = ((bf16[48,80,128]{2,1,0:T(8,128)(2,1)}), bf16[48,80,128]{2,1,0:T(8,128)(2,1)}, u32[]{:S(2)}, u32[]{:S(2)}) async-start(bf16[48,80,128]{2,1,0:T(8,128)(2,1)} %bitcast.9), calls=%async_computation.2 | async-start | bytes 1966080 | tf_op jit(solution)/shard_map/all_to_all | solution.py:625
  69.3 3.1 %collective-permute-start.3 = (bf16[24,80,256]{2,1,0:T(8,128)(2,1)}, bf16[24,80,256]{2,1,0:T(8,128)(2,1)}, u32[]{:S(2)}, u32[]{:S(2)}) collective-permute-start(bf16[24,80,256]{2,1,0:T(8,128)(2,1)} %copy-done.7), channel_id=1, source_target_pairs={{0,1},{1,2},{2,3},{3,4},{4,5},{5,6},{6,7},{7,8},{8,9},{9,10},{10,1... | collective-permute-start | bytes 2949128 | tf_op jit(solution)/shard_map/ppermute | solution.py:617
  72.4 11.2 %collective-permute-start.4 = (bf16[24,80,256]{2,1,0:T(8,128)(2,1)}, bf16[24,80,256]{2,1,0:T(8,128)(2,1)}, u32[]{:S(2)}, u32[]{:S(2)}) collective-permute-start(bf16[24,80,256]{2,1,0:T(8,128)(2,1)} %copy-done.7), channel_id=1, source_target_pairs={{1,0},{2,1},{3,2},{4,3},{5,4},{6,5},{7,6},{8,7},{9,8},{10,9},{11,1... | collective-permute-start | bytes 2949128 | tf_op jit(solution)/shard_map/ppermute | solution.py:618
  83.6 0.1 copy.13
  83.7 0.0 all-gather.3.cloned.1.call-done.points_ref
  83.8 0.0 copy-start.1
  83.8 1.2 copy-done.1
  85.0 17.4 %far_kernels.1 = (bf16[12,128,4096]{2,1,0:T(8,128)(2,1)}, f32[8,128]{1,0:T(8,128)S(1)}) custom-call(s32[24,32]{1,0:T(8,128)S(1)} %broadcast_subtract_fusion.1.list_ref, f32[24,8,128]{2,1,0:T(8,128)S(1)} %copy-done.9, f32[384,8,128]{2,1,0:T(8,128)} %all-gather.3.cloned.1.call-done.points_ref, bf16[48,80,128]{2,1,0:T(8,128)(2,1)S(1)} %bitcast.10), custom_call_target="tpu_custom_call" | custom-call | flops 125829120 | bytes 1000000 | tf_op jit(solution)/shard_map/far_kernels/pallas_call | solution.py:387
  102.4 0.0 all-to-all-done.2
  102.4 1.3 broadcast_add_fusion.after_ref
  103.6 0.3 collective-permute-start.2
  103.9 2.1 %collective-permute-start.1 = (bf16[48,80,128]{2,1,0:T(8,128)(2,1)S(1)}, bf16[48,80,128]{2,1,0:T(8,128)(2,1)S(1)}, u32[]{:S(2)}, u32[]{:S(2)}) collective-permute-start(bf16[48,80,128]{2,1,0:T(8,128)(2,1)S(1)} %broadcast_add_fusion.after_ref), channel_id=1, source_target_pairs={{0,64},{16,80},{32,96},{48,112},{64,0},{80,16},{96,32},{112,48},{1... | collective-permute-start | bytes 2949128 | tf_op jit(solution)/shard_map/ppermute | solution.py:571
  106.1 0.0 collective-permute-start
  106.1 7.9 %collective-permute-done.3.low_ref = bf16[24,80,256]{2,1,0:T(8,128)(2,1)} collective-permute-done((bf16[24,80,256]{2,1,0:T(8,128)(2,1)}, bf16[24,80,256]{2,1,0:T(8,128)(2,1)}, u32[]{:S(2)}, u32[]{:S(2)}) %collective-permute-start.3) | collective-permute-done | bytes 983072 | tf_op jit(solution)/shard_map/ppermute | solution.py:617
  114.0 0.0 collective-permute-done.4.high_ref
  114.0 1.2 copy-done.8
  115.2 34.8 %near_sums.1 = (f32[24,256,64]{2,1,0:T(8,128)S(1)}, f32[8,128]{1,0:T(8,128)S(1)}) custom-call(s32[24,12]{1,0:T(8,128)S(1)} %broadcast_subtract_fusion.list_ref, bf16[24,80,256]{2,1,0:T(8,128)(2,1)} %collective-permute-done.3.low_ref, bf16[24,80,256]{2,1,0:T(8,128)(2,1)S(1)} %copy-done.8, bf16[24,80,256]{2,1,0:T(8,128)(2,1)} %collective-permute-done.4.high_ref, ...), custom_call_target="tpu_custom_call" | custom-call | flops 47185920000 | bytes 6000000 | tf_op jit(solution)/shard_map/near_sums/pallas_call | solution.py:331
  150.0 1.7 copy-done.4
  151.8 0.0 collective-permute-done.2
  151.8 0.0 collective-permute-done.1
  151.8 2.3 %maximum_add_fusion.after_ref.chip_ref = bf16[192,80,128]{2,1,0:T(8,128)(2,1)} fusion(bf16[48,80,128]{2,1,0:T(8,128)(2,1)S(1)} %collective-permute-done.2, bf16[48,80,128]{2,1,0:T(8,128)(2,1)S(1)} %collective-permute-done.1, bf16[48,80,128]{2,1,0:T(8,128)(2,1)S(1)} %collective-permute-done, bf16[48,80,128]{2,1,0:T(8,128)(2,1)S(1)} %broadcast_add_fusion.after_ref, ...), kind=kLoop, calls=%fused_computation | loop fusion | flops 7864320 | bytes 7864576 | tf_op jit(solution)/shard_map/add | solution.py:621
  154.1 0.0 collective-permute-start.5
  154.1 0.0 all-gather.5.cloned.1.call-done.gathered_ref
  154.1 21.8 %far_sums.1 = (f32[24,128,64]{2,1,0:T(8,128)}, f32[8,128]{1,0:T(8,128)}) custom-call(s32[24,32]{1,0:T(8,128)} %copy-done.11, f32[24,8,128]{2,1,0:T(8,128)} %multiply_add_fusion.target_ref, f32[384,8,128]{2,1,0:T(8,128)} %all-gather.3.cloned.1.call-done.points_ref, bf16[384,64,128]{2,1,0:T(8,128)(2,1)} %all-gather.5.cloned.1.call-done.gathered_ref, ...), custom_call_target="tpu_custom_call" | custom-call | flops 31457280000 | bytes 24000000 | tf_op jit(solution)/shard_map/far_sums/pallas_call | solution.py:476
  176.0 0.7 copy-done.13
  176.7 6.9 %upper_sums.1.upper_ref = f32[3,128,64]{2,1,0:T(8,128)S(1)} custom-call(s32[3,32]{1,0:T(4,128)S(1)} %fusion.6.list_ref, bf16[3,8,128]{2,1,0:T(8,128)(2,1)S(1)} %copy-done.12, bf16[192,80,128]{2,1,0:T(8,128)(2,1)} %maximum_add_fusion.after_ref.chip_ref, bf16[192,80,128]{2,1,0:T(8,128)(2,1)} %collective-permute-done.5.across_ref, f32[8,128]{1,0:T(8,128)S(1)} %copy-done.13), custom_call_target="tpu_custom_call" | custom-call | flops 361758720 | bytes 8000000 | tf_op jit(solution)/shard_map/upper_sums/pallas_call | solution.py:524
  183.6 6.1 %final.1 = f32[64,6144]{1,0:T(8,128)} custom-call(f32[24,128,64]{2,1,0:T(8,128)S(1)} %copy-done.6, f32[3,128,64]{2,1,0:T(8,128)S(1)} %upper_sums.1.upper_ref, f32[24,128,128]{2,1,0:T(8,128)S(1)} %copy-done.3, f32[24,256,128]{2,1,0:T(8,128)S(1)} %copy-done, f32[24,256,64]{2,1,0:T(8,128)S(1)} %copy-done.5), custom_call_target="tpu_custom_call" | custom-call | flops 1000000000 | bytes 10000000 | tf_op jit(solution)/shard_map/final/pallas_call | solution.py:559
  (43 shorter events, 0.1 us)
Async XLA Ops:
  6.5 13.0 %copy-start.15 = (f32[8,6144]{1,0:T(8,128)S(1)}, f32[8,6144]{1,0:T(8,128)}, u32[]{:S(2)}) copy-start(f32[8,6144]{1,0:T(8,128)} %points_ref.1) | copy-start | bytes 589828
  6.5 13.0 %copy-start.14 = (f32[64,6144]{1,0:T(8,128)S(1)}, f32[64,6144]{1,0:T(8,128)}, u32[]{:S(2)}) copy-start(f32[64,6144]{1,0:T(8,128)} %weights_ref.1) | copy-start | bytes 4718596
  6.5 77.2 %all-gather.3.cloned.1.call-start = ((), (), s32[]{:S(2)}) async-start(), calls=%async_computation.3 | async-start | bytes 1671168 | tf_op jit(solution)/shard_map/all_gather | solution.py:605
  6.5 0.9 copy-start.16
  7.4 3.6 %copy-start.17 = (bf16[24,8,128]{2,1,0:T(8,128)(2,1)S(1)}, bf16[24,8,128]{2,1,0:T(8,128)(2,1)}, u32[]{:S(2)}) copy-start(bf16[24,8,128]{2,1,0:T(8,128)(2,1)} %param.15) | copy-start | bytes 147460
  11.7 14.2 %all-to-all-start = ((s32[16,1,384]{2,1,0:T(1,128)}), s32[16,1,384]{2,1,0:T(1,128)S(1)}, u32[]{:S(2)}, u32[]{:S(2)}) async-start(s32[16,1,384]{2,1,0:T(1,128)} %get-tuple-element.20), calls=%async_computation | async-start | bytes 49152 | tf_op jit(solution)/shard_map/all_to_all | solution.py:606
  19.5 134.6 %all-gather.5.cloned.1.call-start = ((), (), s32[]{:S(2)}) async-start(), calls=%async_computation.4 | async-start | bytes 6684672 | tf_op jit(solution)/shard_map/all_gather | solution.py:614
  52.8 7.6 %copy-start = (f32[24,256,128]{2,1,0:T(8,128)S(1)}, f32[24,256,128]{2,1,0:T(8,128)}, u32[]{:S(2)}) copy-start(f32[24,256,128]{2,1,0:T(8,128)} %basis_ref.3) | copy-start | bytes 9437188
  52.8 7.7 %copy-start.2 = (f32[24,128,128]{2,1,0:T(8,128)S(1)}, f32[24,128,128]{2,1,0:T(8,128)}, u32[]{:S(2)}) copy-start(f32[24,128,128]{2,1,0:T(8,128)} %transfer_ref.3) | copy-start | bytes 4718596
  60.4 2.5 %copy-start.7 = (bf16[24,80,256]{2,1,0:T(8,128)(2,1)}, bf16[24,80,256]{2,1,0:T(8,128)(2,1)S(1)}, u32[]{:S(2)}) copy-start(bf16[24,80,256]{2,1,0:T(8,128)(2,1)S(1)} %place.1.leaf_ref.own_ref) | copy-start | bytes 2949124
  60.4 3.3 %copy-start.12 = (bf16[3,8,128]{2,1,0:T(8,128)(2,1)S(1)}, bf16[3,8,128]{2,1,0:T(8,128)(2,1)}, u32[]{:S(2)}) copy-start(bf16[3,8,128]{2,1,0:T(8,128)(2,1)} %own_ref.1) | copy-start | bytes 18436
  60.4 23.2 %copy-start.19 = (s32[24,12]{0,1:T(8,128)S(1)}, s32[24,12]{0,1:T(8,128)}, u32[]{:S(2)}) copy-start(s32[24,12]{0,1:T(8,128)} %param.17) | copy-start | bytes 3460
  60.5 23.3 %copy-start.18 = (s32[24,32]{1,0:T(8,128)S(1)}, s32[24,32]{1,0:T(8,128)}, u32[]{:S(2)}) copy-start(s32[24,32]{1,0:T(8,128)} %param.18) | copy-start | bytes 9220
  60.5 23.3 %copy-start.9 = (f32[24,8,128]{2,1,0:T(8,128)S(1)}, f32[24,8,128]{2,1,0:T(8,128)}, u32[]{:S(2)}) copy-start(f32[24,8,128]{2,1,0:T(8,128)} %multiply_add_fusion.target_ref) | copy-start | bytes 294916
  62.9 0.7 copy-start.10
  64.9 37.4 %all-to-all-start.2 = ((bf16[48,80,128]{2,1,0:T(8,128)(2,1)}), bf16[48,80,128]{2,1,0:T(8,128)(2,1)}, u32[]{:S(2)}, u32[]{:S(2)}) async-start(bf16[48,80,128]{2,1,0:T(8,128)(2,1)} %bitcast.9), calls=%async_computation.2 | async-start | bytes 1966080 | tf_op jit(solution)/shard_map/all_to_all | solution.py:625
  69.3 44.7 %collective-permute-start.3 = (bf16[24,80,256]{2,1,0:T(8,128)(2,1)}, bf16[24,80,256]{2,1,0:T(8,128)(2,1)}, u32[]{:S(2)}, u32[]{:S(2)}) collective-permute-start(bf16[24,80,256]{2,1,0:T(8,128)(2,1)} %copy-done.7), channel_id=1, source_target_pairs={{0,1},{1,2},{2,3},{3,4},{4,5},{5,6},{6,7},{7,8},{8,9},{9,10},{10,1... | collective-permute-start | bytes 2949128 | tf_op jit(solution)/shard_map/ppermute | solution.py:617
  72.4 41.6 %collective-permute-start.4 = (bf16[24,80,256]{2,1,0:T(8,128)(2,1)}, bf16[24,80,256]{2,1,0:T(8,128)(2,1)}, u32[]{:S(2)}, u32[]{:S(2)}) collective-permute-start(bf16[24,80,256]{2,1,0:T(8,128)(2,1)} %copy-done.7), channel_id=1, source_target_pairs={{1,0},{2,1},{3,2},{4,3},{5,4},{6,5},{7,6},{8,7},{9,8},{10,9},{11,1... | collective-permute-start | bytes 2949128 | tf_op jit(solution)/shard_map/ppermute | solution.py:618
  83.7 66.2 %copy-start.11 = (s32[24,32]{1,0:T(8,128)}, s32[24,32]{1,0:T(8,128)S(1)}, u32[]{:S(2)}) copy-start(s32[24,32]{1,0:T(8,128)S(1)} %broadcast_subtract_fusion.1.list_ref) | copy-start | bytes 9220
  83.8 1.2 copy-start.1
  103.6 48.1 %collective-permute-start.2 = (bf16[48,80,128]{2,1,0:T(8,128)(2,1)S(1)}, bf16[48,80,128]{2,1,0:T(8,128)(2,1)S(1)}, u32[]{:S(2)}, u32[]{:S(2)}) collective-permute-start(bf16[48,80,128]{2,1,0:T(8,128)(2,1)S(1)} %broadcast_add_fusion.after_ref), channel_id=1, source_target_pairs={{0,32},{16,48},{32,64},{48,80},{64,96},{80,112},{96,0},{112,16},{1... | collective-permute-start | bytes 2949128 | tf_op jit(solution)/shard_map/ppermute | solution.py:571
  103.9 47.8 %collective-permute-start.1 = (bf16[48,80,128]{2,1,0:T(8,128)(2,1)S(1)}, bf16[48,80,128]{2,1,0:T(8,128)(2,1)S(1)}, u32[]{:S(2)}, u32[]{:S(2)}) collective-permute-start(bf16[48,80,128]{2,1,0:T(8,128)(2,1)S(1)} %broadcast_add_fusion.after_ref), channel_id=1, source_target_pairs={{0,64},{16,80},{32,96},{48,112},{64,0},{80,16},{96,32},{112,48},{1... | collective-permute-start | bytes 2949128 | tf_op jit(solution)/shard_map/ppermute | solution.py:571
  106.1 45.7 %collective-permute-start = (bf16[48,80,128]{2,1,0:T(8,128)(2,1)S(1)}, bf16[48,80,128]{2,1,0:T(8,128)(2,1)S(1)}, u32[]{:S(2)}, u32[]{:S(2)}) collective-permute-start(bf16[48,80,128]{2,1,0:T(8,128)(2,1)S(1)} %broadcast_add_fusion.after_ref), channel_id=1, source_target_pairs={{0,96},{16,112},{32,0},{48,16},{64,32},{80,48},{96,64},{112,80},{1... | collective-permute-start | bytes 2949128 | tf_op jit(solution)/shard_map/ppermute | solution.py:571
  114.0 1.2 copy-start.8
  150.0 1.8 copy-start.4
  151.7 2.3 %copy-start.20 = (s32[3,32]{1,0:T(4,128)S(1)}, s32[3,32]{1,0:T(4,128)}, u32[]{:S(2)}) copy-start(s32[3,32]{1,0:T(4,128)} %param.19) | copy-start | bytes 1156
  154.1 21.9 %collective-permute-start.5 = (bf16[192,80,128]{2,1,0:T(8,128)(2,1)}, bf16[192,80,128]{2,1,0:T(8,128)(2,1)}, u32[]{:S(2)}, u32[]{:S(2)}) collective-permute-start(bf16[192,80,128]{2,1,0:T(8,128)(2,1)} %maximum_add_fusion.after_ref.chip_ref), channel_id=1, source_target_pairs={{0,16},{16,0},{32,48},{48,32},{64,80},{80,64},{96,112},{112,96},{1... | collective-permute-start | bytes 11796488 | tf_op jit(solution)/shard_map/ppermute | solution.py:571
  176.0 0.7 copy-start.13
  176.6 6.9 %copy-start.3 = (f32[24,128,128]{2,1,0:T(8,128)S(1)}, f32[24,128,128]{2,1,0:T(8,128)}, u32[]{:S(2)}) copy-start(f32[24,128,128]{2,1,0:T(8,128)} %transfer_ref.3) | copy-start | bytes 4718596
  176.6 6.9 %copy-start.5 = (f32[24,256,64]{2,1,0:T(8,128)S(1)}, f32[24,256,64]{2,1,0:T(8,128)}, u32[]{:S(2)}) copy-start(f32[24,256,64]{2,1,0:T(8,128)} %copy-done.4) | copy-start | bytes 4718596
  176.7 6.9 %copy-start.6 = (f32[24,128,64]{2,1,0:T(8,128)S(1)}, f32[24,128,64]{2,1,0:T(8,128)}, u32[]{:S(2)}) copy-start(f32[24,128,64]{2,1,0:T(8,128)} %get-tuple-element.26.far_ref) | copy-start | bytes 2359300
Sparse Core Ops, SparseCore 0:
  11.8 48.9 all-gather.2
  63.8 86.7 all-gather.4
